TPU v7x, 256 devices: a whole 4x4x8 slice. The times are simulated.
256 devices in a mesh: seq: 64 (over z, y, core), dp: 4 (over x).
Axes of the slice: x: 4, y: 4, z: 8, core: 2. Of those that a mesh axis runs over, the one named last changes fastest.
Arguments:
- queries: bfloat16 [262144, 128], P(('dp', 'seq')), parts along dimension 0, may hold values from -150 to 150
- key_rows: bfloat16 [262144, 128], P(('dp', 'seq')), parts along dimension 0, may hold values from -5 to 5
- values: bfloat16 [262144, 128], P(('dp', 'seq')), parts along dimension 0, may hold values from -6 to 6
- out_grad: bfloat16 [262144, 128], P(('dp', 'seq')), parts along dimension 0, may hold values from -6 to 6
- cluster_id: int32 [4, 65536], P('dp', 'seq'), parts along dimension 0, may hold values from 0 to 1023, as said below
- cluster_owner: int32 [4, 1024], P('dp'), parts along dimension 0, may hold values from 0 to 1023, as said below
- old_centroids: float32 [4, 1024, 128], P('dp', 'seq'), parts along dimension 0, may hold values from -0.6 to 0.6
Outputs:
- attn_out: bfloat16 [262144, 128], P(('dp', 'seq')), parts along dimension 0
- grad_queries: bfloat16 [262144, 128], P(('dp', 'seq')), parts along dimension 0
- grad_keys: bfloat16 [262144, 128], P(('dp', 'seq')), parts along dimension 0
- grad_values: bfloat16 [262144, 128], P(('dp', 'seq')), parts along dimension 0
- new_centroids: float32 [4, 1024, 128], P('dp', 'seq'), parts along dimension 0
There are 4 independent parts, one for each index of `dp`. A program takes and returns all parts, laid end to end along the dimension named above; each array names one. Nothing has to cross between parts.
Inputs may be any that keep to these rules, and one draw needn't show every extreme that they name: `cluster_id`: each cluster holds 128 tokens at most and 16 at least; the 16 clusters of one owner hold 1024 tokens together, and each owner has a cluster of exactly 128. The 1024 tokens of one device name clusters of one owner at most 32 times per head, and every device reaches that for some owner. `cluster_owner`: each head's row is a permutation; value v puts the cluster on device v // 16 of seq as its cluster v % 16.
All inputs are finite; a program needn't handle non-finite values.
Results may differ from a plain program's by a relative error of at most 0.0056.
Values may be sent and summed in bfloat16 or wider, within the bound.
A program may use at most 64 MiB of HBM per device.

v0:
```python
import math

import jax
import jax.numpy as jnp
from jax import lax
from jax.sharding import PartitionSpec as P

CL_DEV = 16
CAP = 128


def running_count(onehot):
    rows_n, cols_n = onehot.shape
    block_len = math.gcd(rows_n, 512)
    block_num = rows_n // block_len
    lower_tri = (jnp.arange(block_len)[:, None] >= jnp.arange(block_len)[None, :]).astype(
        jnp.bfloat16
    )
    blocks = onehot.astype(jnp.bfloat16).reshape(block_num, block_len, cols_n)
    inner = jnp.einsum("ij,njm->nim", lower_tri, blocks, preferred_element_type=jnp.float32)
    totals = inner[:, -1]
    offsets = jnp.cumsum(totals, axis=0) - totals
    return (inner + offsets[:, None]).reshape(rows_n, cols_n).astype(jnp.int32)


def slot_sources(inclusive, room):
    ranks = jnp.arange(room, dtype=jnp.int32)
    return jnp.sum(
        (inclusive.T[:, None, :] <= ranks[None, :, None]).astype(jnp.int32), axis=-1
    ).reshape(-1)


def masked_scores(query_c, key_c, place_c, doc_tokens):
    score_scale = 1.0 / math.sqrt(query_c.shape[-1])
    scores = (
        jnp.einsum("hqd,hkd->hqk", query_c, key_c, preferred_element_type=jnp.float32) * score_scale
    )
    query_pos = place_c[..., :, None]
    key_pos = place_c[..., None, :]
    width_cap = place_c.shape[-1]
    diagonal = jnp.arange(width_cap)[:, None] == jnp.arange(width_cap)[None, :]
    allowed = (key_pos <= query_pos) & (query_pos < doc_tokens) | diagonal
    return (jnp.where(allowed, scores, jnp.float32(-1e30)), allowed)


def take_rows(table, where, fill):
    return jnp.take(table, where, axis=0, mode="fill", fill_value=fill)


def shards(queries, key_rows, values, out_grad, cluster_id, cluster_owner, old_centroids):
    seq_count = lax.axis_size("seq")
    tok_rows = queries.shape[0]
    head_count = cluster_id.shape[0]
    head_width = queries.shape[1] // head_count
    send_room = 2 * tok_rows // seq_count
    slot_total = seq_count * send_room
    doc_tokens = tok_rows * seq_count
    cluster_total = cluster_owner.shape[1]
    score_scale = 1.0 / math.sqrt(head_width)
    owner_value = jnp.take_along_axis(cluster_owner, cluster_id, axis=1)
    target = owner_value // CL_DEV
    local_cluster = owner_value % CL_DEV
    position = lax.axis_index("seq") * tok_rows + jnp.arange(tok_rows, dtype=jnp.int32)

    def send_plan(target_h):
        member = (target_h[:, None] == jnp.arange(seq_count, dtype=jnp.int32)[None, :]).astype(
            jnp.int32
        )
        inclusive = running_count(member)
        before = jnp.sum(inclusive * member, axis=-1) - 1
        return (target_h * send_room + before, slot_sources(inclusive, send_room))

    send_place, send_source = jax.vmap(send_plan)(target)
    joined_in = jnp.concatenate(
        [
            item.reshape(tok_rows, head_count, head_width)
            for item in (queries, key_rows, values, out_grad)
        ],
        axis=-1,
    )
    rows_heads = joined_in.transpose(1, 0, 2)
    send_rows = jax.vmap(lambda rows_h, src_h: take_rows(rows_h, src_h, 0))(rows_heads, send_source)
    send_rows = send_rows.reshape(head_count, seq_count, send_room, 4 * head_width)
    send_local = jax.vmap(lambda loc_h, src_h: take_rows(loc_h, src_h, CL_DEV))(
        local_cluster, send_source
    )
    send_pos = jax.vmap(lambda src_h: take_rows(position, src_h, doc_tokens))(send_source)
    send_meta = (
        jnp.stack([send_local, send_pos], axis=1)
        .reshape(head_count, 2, seq_count, send_room)
        .transpose(0, 2, 1, 3)
    )

    def forward_one(item):
        rows_c, place_c = item
        query_c = rows_c[..., 0:head_width]
        key_c = rows_c[..., head_width : 2 * head_width]
        value_c = rows_c[..., 2 * head_width : 3 * head_width]
        scores, allowed = masked_scores(query_c, key_c, place_c, doc_tokens)
        peak = jnp.max(scores, axis=-1, keepdims=True)
        weights = jnp.where(allowed, jnp.exp(scores - peak), jnp.float32(0.0))
        total = jnp.sum(weights, axis=-1, keepdims=True)
        probs_low = (weights / total).astype(jnp.bfloat16)
        attn_low = jnp.einsum(
            "hqk,hkd->hqd", probs_low, value_c, preferred_element_type=jnp.float32
        ).astype(jnp.bfloat16)
        return (attn_low, peak, total)

    def backward_one(item):
        rows_c, place_c, attn_low, peak, total = item
        query_c = rows_c[..., 0:head_width]
        key_c = rows_c[..., head_width : 2 * head_width]
        value_c = rows_c[..., 2 * head_width : 3 * head_width]
        grad_c = rows_c[..., 3 * head_width : 4 * head_width]
        scores, allowed = masked_scores(query_c, key_c, place_c, doc_tokens)
        probs = jnp.where(allowed, jnp.exp(scores - peak), jnp.float32(0.0)) / total
        probs_low = probs.astype(jnp.bfloat16)
        delta = jnp.sum(grad_c.astype(jnp.float32) * attn_low.astype(jnp.float32), axis=-1)
        dprobs = jnp.einsum("hqd,hkd->hqk", grad_c, value_c, preferred_element_type=jnp.float32)
        dscores = (probs * (dprobs - delta[..., None]) * score_scale).astype(jnp.bfloat16)
        grad_query = jnp.einsum(
            "hqk,hkd->hqd", dscores, key_c, preferred_element_type=jnp.float32
        ).astype(jnp.bfloat16)
        grad_key = jnp.einsum(
            "hqk,hqd->hkd", dscores, query_c, preferred_element_type=jnp.float32
        ).astype(jnp.bfloat16)
        grad_value = jnp.einsum(
            "hqk,hqd->hkd", probs_low, grad_c, preferred_element_type=jnp.float32
        ).astype(jnp.bfloat16)
        return jnp.concatenate([grad_query, grad_key, grad_value], axis=-1)

    rows_in = lax.all_to_all(send_rows, "seq", split_axis=1, concat_axis=1, tiled=True)
    meta_in = lax.all_to_all(send_meta, "seq", split_axis=1, concat_axis=1, tiled=True)
    part_heads = rows_in.shape[0]
    flat_rows = rows_in.reshape(part_heads, slot_total, 4 * head_width)
    local_in = meta_in[:, :, 0].reshape(part_heads, slot_total)
    place_in = meta_in[:, :, 1].reshape(part_heads, slot_total)

    def owner_plan(local_h):
        owned = (local_h[:, None] == jnp.arange(CL_DEV, dtype=jnp.int32)[None, :]).astype(jnp.int32)
        inclusive = running_count(owned)
        within = jnp.sum(inclusive * owned, axis=-1) - 1
        target_row = jnp.where(local_h < CL_DEV, local_h * CAP + within, CL_DEV * CAP)
        return (
            target_row,
            slot_sources(inclusive, CAP),
            jnp.sum(owned, axis=0).astype(jnp.float32),
        )

    target_row, cluster_source, owned_count = jax.vmap(owner_plan)(local_in)
    layout = jax.vmap(lambda rows_h, src_h: take_rows(rows_h, src_h, 0))(flat_rows, cluster_source)
    layout = layout.reshape(part_heads, CL_DEV, CAP, 4 * head_width)
    places = jax.vmap(lambda place_h, src_h: take_rows(place_h, src_h, doc_tokens))(
        place_in, cluster_source
    )
    places = places.reshape(part_heads, CL_DEV, CAP)
    rows_major = layout.transpose(1, 0, 2, 3)
    places_major = places.transpose(1, 0, 2)
    attn_major, peaks, totals = lax.map(forward_one, (rows_major, places_major))
    grads_major = lax.map(backward_one, (rows_major, places_major, attn_major, peaks, totals))
    results_major = jnp.concatenate([attn_major, grads_major], axis=-1)
    width_out = results_major.shape[-1]
    flat = results_major.transpose(1, 0, 2, 3).reshape(part_heads, CL_DEV * CAP, width_out)
    picked = jax.vmap(lambda flat_h, where_h: take_rows(flat_h, where_h, 0))(flat, target_row)
    returned_rows = lax.all_to_all(
        picked.reshape(part_heads, seq_count, send_room, width_out),
        "seq",
        split_axis=1,
        concat_axis=1,
        tiled=True,
    )
    key_heads = key_rows.reshape(tok_rows, head_count, head_width).transpose(1, 0, 2)
    cluster_onehot = (
        owner_value[:, None, :] == jnp.arange(cluster_total, dtype=jnp.int32)[None, :, None]
    ).astype(jnp.bfloat16)
    all_sums = jnp.einsum(
        "hct,htd->hcd", cluster_onehot, key_heads, preferred_element_type=jnp.float32
    )
    all_counts = jnp.sum(cluster_onehot, axis=-1, dtype=jnp.float32)
    key_sum, member_count = (
        lax.psum_scatter(all_sums, "seq", scatter_dimension=1, tiled=True),
        lax.psum_scatter(all_counts, "seq", scatter_dimension=1, tiled=True),
    )
    flat_back = returned_rows.reshape(head_count, slot_total, 4 * head_width)
    mine = jax.vmap(lambda back_h, where_h: jnp.take(back_h, where_h, axis=0))(
        flat_back, send_place
    )
    outputs = [
        mine[..., j * head_width : (j + 1) * head_width]
        .transpose(1, 0, 2)
        .reshape(tok_rows, head_count * head_width)
        for j in range(4)
    ]
    blended = 0.5 * old_centroids + 0.5 * key_sum / member_count[..., None]
    new_centroids = blended * lax.rsqrt(jnp.mean(blended * blended, axis=-1, keepdims=True) + 1e-06)
    return (outputs[0], outputs[1], outputs[2], outputs[3], new_centroids)


def solution(mesh):
    return jax.shard_map(
        shards,
        mesh=mesh,
        in_specs=(
            P(("dp", "seq"), None),
            P(("dp", "seq"), None),
            P(("dp", "seq"), None),
            P(("dp", "seq"), None),
            P("dp", "seq"),
            P("dp", None),
            P("dp", "seq", None),
        ),
        out_specs=(
            P(("dp", "seq"), None),
            P(("dp", "seq"), None),
            P(("dp", "seq"), None),
            P(("dp", "seq"), None),
            P("dp", "seq", None),
        ),
        check_vma=False,
    )
```

profile of v0, /device:TPU:1, one launch (start us, length us, event | category | flops | bytes accessed | tf_op | source)
XLA Modules:
  0.0 432.4 jit_solution(11266685244374335885)
XLA Ops:
  7.2 0.7 compare_select_fusion.7
  7.9 4.5 %gather_fusion = s32[1024]{0:T(1024)S(1)} fusion(s32[1024]{0:T(1024)S(1)} %bitcast.225, s32[1024]{0:T(1024)S(1)} %broadcast_clamp_fusion.1), kind=kCustom, calls=%fused_computation.2 | custom fusion | bytes 12288 | tf_op jit(solution)/shard_map/jit(take_along_axis)/gather | solution.py:60
  13.0 0.7 fusion.66
  14.3 1.2 convert_reduce_fusion.1
  15.7 12.5 %gather_fusion.2 = s32[2048]{0:T(1024)S(1)} fusion(s32[1,1024]{1,0:T(1,128)S(1)} %get-tuple-element.174, s32[2048]{0:T(1024)S(1)} %bitcast.226), kind=kCustom, calls=%fused_computation.4 | custom fusion | bytes 32768 | tf_op jit(solution)/shard_map/vmap(jit(_take))/gather | solution.py:47
  28.3 8.6 %gather_fusion.1 = s32[2048]{0:T(1024)S(1)} fusion(s32[1024]{0:T(1024)S(1)} %iota_add_fusion, s32[2048]{0:T(1024)S(1)} %broadcast_clamp_fusion), kind=kCustom, calls=%fused_computation.3 | custom fusion | bytes 24576 | tf_op jit(solution)/shard_map/vmap(jit(_take))/gather | solution.py:47
  37.0 0.7 copy.34
  37.7 13.2 %all-to-all-start = ((s32[1,64,2,32]{3,2,0,1:T(2,128)}), s32[1,64,2,32]{3,2,0,1:T(2,128)S(1)}, u32[]{:S(2)}, u32[]{:S(2)}) async-start(s32[1,64,2,32]{3,2,0,1:T(2,128)} %copy.34), calls=%async_computation | async-start | bytes 131072 | tf_op jit(solution)/shard_map/all_to_all | solution.py:133
  51.0 11.7 %gather_fusion.4 = bf16[2048,512]{1,0:T(8,128)(2,1)S(1)} fusion(bf16[1,1024,512]{2,1,0:T(8,128)(2,1)S(1)} %maximum_bitcast_fusion.1, s32[2048]{0:T(1024)S(1)} %bitcast.227), kind=kCustom, calls=%fused_computation.6 | custom fusion | bytes 4210688 | tf_op jit(solution)/shard_map/vmap(jit(_take))/gather | solution.py:47
  62.7 1.6 broadcast_select_fusion
  64.3 10.3 %all-to-all-start.1 = ((bf16[1,64,32,512]{3,2,0,1:T(8,128)(2,1)}), bf16[1,64,32,512]{3,2,0,1:T(8,128)(2,1)S(1)}, u32[]{:S(2)}, u32[]{:S(2)}) async-start(bf16[1,64,32,512]{3,2,0,1:T(8,128)(2,1)} %broadcast_select_fusion), calls=%async_computation.1 | async-start | bytes 4194304 | tf_op jit(solution)/shard_map/all_to_all | solution.py:132
  76.0 2.0 convert_reduce_fusion
  78.1 12.5 %gather_fusion.3 = s32[2048]{0:T(1024)S(1)} fusion(s32[1,2048]{1,0:T(1,128)S(1)} %reshape_squeeze.4, s32[2048]{0:T(1024)S(1)} %bitcast.232), kind=kCustom, calls=%fused_computation.5 | custom fusion | bytes 32768 | tf_op jit(solution)/shard_map/vmap(jit(_take))/gather | solution.py:47
  90.9 33.5 %all-to-all-done.1 = bf16[1,64,32,512]{3,2,0,1:T(8,128)(2,1)S(1)} async-done(((bf16[1,64,32,512]{3,2,0,1:T(8,128)(2,1)}), bf16[1,64,32,512]{3,2,0,1:T(8,128)(2,1)S(1)}, u32[]{:S(2)}, u32[]{:S(2)}) %all-to-all-start.1) | async-done | bytes 2097184 | tf_op jit(solution)/shard_map/all_to_all | solution.py:132
  124.3 21.6 %gather_fusion.6 = bf16[2048,512]{1,0:T(8,128)(2,1)} fusion(bf16[1,2048,512]{2,1,0:T(8,128)(2,1)S(1)} %bitcast.228, s32[2048]{0:T(1024)S(1)} %bitcast.231), kind=kCustom, calls=%fused_computation.clone | custom fusion | bytes 4210688 | tf_op jit(solution)/shard_map/vmap(jit(_take))/gather | solution.py:47
  145.9 1.8 bitcast_select_fusion.1
  147.7 10.2 %while.24 = (s32[]{:T(128)}, bf16[16,1,128,128]{3,2,1,0:T(8,128)(2,1)S(1)}, f32[16,1,128,1]{2,3,1,0:T(1,128)S(1)}, f32[16,1,128,1]{2,3,1,0:T(1,128)S(1)}, s32[16...) while((s32[]{:T(128)}, bf16[16,1,128,128]{3,2,1,0:T(8,128)(2,1)S(1)}, ...), condition=%wide.region_8.10_spmd, body=%wide.region_5.9_spmd.sunk | while | flops 8765314 | bytes 599389 | solution.py:159
  158.2 28.9 %while.25 = (s32[]{:T(128)}, bf16[16,1,128,384]{2,3,1,0:T(8,128)(2,1)}, s32[16,1,128]{2,1,0:T(1,128)S(1)}, bf16[16,1,128,512]{3,2,1,0:T(8,128)(2,1)S(1)}, f32[16...) while((s32[]{:T(128)}, ...), condition=%wide.region_11.13_spmd, body=%wide.region_9.12_spmd.sunk | while | flops 21610496 | bytes 1154277 | solution.py:160
  163.0 0.7 fusion.104
  172.0 0.7 fusion.104
  187.1 3.0 pad_maximum_fusion
  190.0 2.9 copy.42
  192.9 21.6 %gather_fusion.7 = bf16[2048,512]{1,0:T(8,128)(2,1)} fusion(bf16[1,2048,512]{2,1,0:T(8,128)(2,1)S(1)} %bitcast.229, s32[2048]{0:T(1024)S(1)} %bitcast.230), kind=kCustom, calls=%fused_computation.1.clone | custom fusion | bytes 4210688 | tf_op jit(solution)/shard_map/vmap(jit(_take))/gather | solution.py:47
  214.5 2.8 bitcast_select_fusion
  217.3 7.2 %all-to-all-start.2 = ((bf16[1,64,32,512]{3,2,0,1:T(8,128)(2,1)}), bf16[1,64,32,512]{3,2,0,1:T(8,128)(2,1)S(1)}, u32[]{:S(2)}, u32[]{:S(2)}) async-start(bf16[1,64,32,512]{3,2,0,1:T(8,128)(2,1)} %bitcast.236), calls=%async_computation.2 | async-start | bytes 4194304 | tf_op jit(solution)/shard_map/all_to_all | solution.py:165
  224.5 1.6 fusion.36
  227.9 160.4 %all-reduce.1 = f32[1,1024]{1,0:T(1,128)S(1)} all-reduce(f32[1,1024]{1,0:T(1,128)S(1)} %bitcast.261), channel_id=3, replica_groups=mesh['seq'=64,'dp'=4] {'seq'}, use_global_device_ids=true, to_apply=%region_15.17.clone | all-reduce | flops 1024 | bytes 8192
  388.6 28.0 %all-reduce.4.cloned.1.call-done = f32[1,1024,128]{2,1,0:T(8,128)} async-done(((f32[1,1024,128]{2,1,0:T(8,128)}), f32[1,1024,128]{2,1,0:T(8,128)}) %all-reduce.4.cloned.1.call-update) | async-done | bytes 524304
  416.6 0.9 multiply_reduce_fusion.1
  417.5 0.7 broadcast_multiply_fusion
  418.1 6.1 %gather_fusion.5 = bf16[1024,512]{1,0:T(8,128)(2,1)S(1)} fusion(bf16[1,2048,512]{2,1,0:T(8,128)(2,1)S(1)} %bitcast.234, s32[1024]{0:T(1024)S(1)} %bitcast.233), kind=kCustom, calls=%fused_computation.7 | custom fusion | bytes 2105344 | tf_op jit(solution)/shard_map/vmap(jit(_take))/gather | solution.py:185
  424.5 1.1 slice_bitcast_fusion.14
  (336 shorter events, 41.3 us)
Async XLA Ops:
  7.2 0.7 copy-start
  7.9 4.6 %copy-start.6 = (s32[1,1024]{1,0:T(1,128)S(1)}, s32[1,1024]{1,0:T(1,128)}, u32[]{:S(2)}) copy-start(s32[1,1024]{1,0:T(1,128)} %param.17) | copy-start | bytes 12292
  28.2 22.6 %copy-start.1 = (bf16[1024,128]{1,0:T(8,128)(2,1)S(1)}, bf16[1024,128]{1,0:T(8,128)(2,1)}, u32[]{:S(2)}) copy-start(bf16[1024,128]{1,0:T(8,128)(2,1)} %param.16) | copy-start | bytes 786436
  28.3 22.6 %copy-start.2 = (bf16[1024,128]{1,0:T(8,128)(2,1)S(1)}, bf16[1024,128]{1,0:T(8,128)(2,1)}, u32[]{:S(2)}) copy-start(bf16[1024,128]{1,0:T(8,128)(2,1)} %param.15) | copy-start | bytes 786436
  28.3 22.6 %copy-start.3 = (bf16[1024,128]{1,0:T(8,128)(2,1)S(1)}, bf16[1024,128]{1,0:T(8,128)(2,1)}, u32[]{:S(2)}) copy-start(bf16[1024,128]{1,0:T(8,128)(2,1)} %param.13) | copy-start | bytes 786436
  28.3 22.6 %copy-start.4 = (bf16[1024,128]{1,0:T(8,128)(2,1)S(1)}, bf16[1024,128]{1,0:T(8,128)(2,1)}, u32[]{:S(2)}) copy-start(bf16[1024,128]{1,0:T(8,128)(2,1)} %param.14) | copy-start | bytes 786436
  37.7 26.7 %all-to-all-start = ((s32[1,64,2,32]{3,2,0,1:T(2,128)}), s32[1,64,2,32]{3,2,0,1:T(2,128)S(1)}, u32[]{:S(2)}, u32[]{:S(2)}) async-start(s32[1,64,2,32]{3,2,0,1:T(2,128)} %copy.34), calls=%async_computation | async-start | bytes 131072 | tf_op jit(solution)/shard_map/all_to_all | solution.py:133
  64.3 60.0 %all-to-all-start.1 = ((bf16[1,64,32,512]{3,2,0,1:T(8,128)(2,1)}), bf16[1,64,32,512]{3,2,0,1:T(8,128)(2,1)S(1)}, u32[]{:S(2)}, u32[]{:S(2)}) async-start(bf16[1,64,32,512]{3,2,0,1:T(8,128)(2,1)} %broadcast_select_fusion), calls=%async_computation.1 | async-start | bytes 4194304 | tf_op jit(solution)/shard_map/all_to_all | solution.py:132
  217.3 7.2 %copy-start.5 = (bf16[1024,128]{1,0:T(8,128)(2,1)S(1)}, bf16[1024,128]{1,0:T(8,128)(2,1)}, u32[]{:S(2)}) copy-start(bf16[1024,128]{1,0:T(8,128)(2,1)} %param.14) | copy-start | bytes 786436
  217.3 200.8 %all-to-all-start.2 = ((bf16[1,64,32,512]{3,2,0,1:T(8,128)(2,1)}), bf16[1,64,32,512]{3,2,0,1:T(8,128)(2,1)S(1)}, u32[]{:S(2)}, u32[]{:S(2)}) async-start(bf16[1,64,32,512]{3,2,0,1:T(8,128)(2,1)} %bitcast.236), calls=%async_computation.2 | async-start | bytes 4194304 | tf_op jit(solution)/shard_map/all_to_all | solution.py:165
  224.5 1.7 copy-start.8
  224.5 192.1 %copy-start.7 = (f32[1,16,128]{2,1,0:T(8,128)S(1)}, f32[1,16,128]{2,1,0:T(8,128)}, u32[]{:S(2)}) copy-start(f32[1,16,128]{2,1,0:T(8,128)} %param.19) | copy-start | bytes 24580
  224.5 192.1 %all-reduce.4.cloned.1.call-start = ((), (), s32[]{:S(2)}) async-start(), calls=%async_computation.3 | async-start | bytes 1048576
Sparse Core Ops, SparseCore 0:
  228.8 187.6 all-reduce.3
where the time goes:
time: 434 us; the launch traced here: 432 us
  blocking collectives  160 us (37%)
  local copies, waits for them, and re-layouts  107 us (25%)
  waiting for transfers between devices  61.5 us (14%)
  other arithmetic  31.6 us (7%)
  starting transfers between devices  30.7 us (7%)
  matrix products  24.7 us (6%)
  between operations  15.2 us (4%)
    unnamed x1, blocking collectives  160 us
    gather x12, local copies, waits for them, and re-layouts, take_rows(): return jnp.take(table, where, axis=0, mode='fill', fill_value=fill)  88.6 us
    all_to_all x1, waiting for transfers between devices, shards(): lax.all_to_all(send_rows, 'seq', split_axis=1, concat_axis=1, tiled=True)  33.5 us
    unnamed x2, waiting for transfers between devices  28 us
    all_to_all x1, starting transfers between devices, shards(): lax.all_to_all(send_meta, 'seq', split_axis=1, concat_axis=1, tiled=True)  13.2 us
    dynamic_update_slice x16, other arithmetic, shards(): lax.map(backward_one, (rows_major, places_major, attn_major, peaks, totals))  10.3 us
    all_to_all x1, starting transfers between devices, shards(): lax.all_to_all(send_rows, 'seq', split_axis=1, concat_axis=1, tiled=True)  10.3 us
  transfers between devices with their start and end apart: 4, of which 2 were waited for; matrix products, arithmetic and copies ran while one was open for 8% of the time, Pallas kernels for 0%

commit v1 on v0

v1 whole, which is shorter than its diff:
```python
import functools
import math

import jax
import jax.numpy as jnp
from jax import lax
from jax.experimental import pallas as pl
from jax.experimental.pallas import tpu as pltpu
from jax.sharding import PartitionSpec as P

MESH = pl.DeviceIdType.MESH
HD = 128
CL_DEV = 16
TOK = 1024
DEVS = 64
ROOM = 32
PLANE = 8
PLANES = DEVS // PLANE
CHUNK = PLANE * ROOM
BLOCKS = TOK // 128
ORDER = (4, 1, 7, 3, 5, 2, 6, 0)
BF16 = jnp.bfloat16
F32 = jnp.float32


def dot(a, b):
    return jnp.dot(a, b, preferred_element_type=F32)


def dot_nt(a, b):
    return lax.dot_general(a, b, (((1,), (1,)), ((), ())), preferred_element_type=F32)


def dot_tn(a, b):
    return lax.dot_general(a, b, (((0,), (0,)), ((), ())), preferred_element_type=F32)


def iota(shape, dim):
    return lax.broadcasted_iota(jnp.int32, shape, dim).astype(F32)


def onehot(mask):
    return jnp.where(mask, 1.0, 0.0).astype(BF16)


def prefix_and_total():
    row = lax.broadcasted_iota(jnp.int32, (128, 256), 0)
    col = lax.broadcasted_iota(jnp.int32, (128, 256), 1)
    return onehot((row < col) | (col >= 128))


def token_slots(cluster_id, owner):
    ident = cluster_id[...]
    low = onehot(lax.broadcasted_iota(jnp.int32, (128, TOK), 0) == lax.rem(ident, 128))
    table = jnp.concatenate([owner[:, 128 * b : 128 * (b + 1)] for b in range(8)], axis=0)
    table_dev = lax.div(table, CL_DEV)
    table_loc = table - table_dev * CL_DEV
    tables = jnp.concatenate([table_dev, table_loc], axis=0).astype(F32).astype(BF16)
    found = dot(tables, low)
    high = lax.broadcasted_iota(jnp.int32, (8, TOK), 0) == lax.div(ident, 128)
    target = jnp.sum(jnp.where(high, found[:8], 0.0), axis=0, keepdims=True)
    local = jnp.sum(jnp.where(high, found[8:], 0.0), axis=0, keepdims=True)
    device = iota((DEVS, 128), 0)
    members = [device == target[:, 128 * b : 128 * (b + 1)] for b in range(BLOCKS)]
    counted = dot(jnp.concatenate([onehot(m) for m in members], axis=0), prefix_and_total())
    running = jnp.zeros((DEVS, 128), F32)
    ranks = []
    for b in range(BLOCKS):
        part = counted[DEVS * b : DEVS * (b + 1)]
        ranks.append(
            jnp.sum(jnp.where(members[b], part[:, :128] + running, 0.0), axis=0, keepdims=True)
        )
        running = running + part[:, 128:]
    rank = jnp.concatenate(ranks, axis=1)
    return target, local, rank


def turned(rows):
    n = rows.shape[0]
    return jnp.concatenate([rows, jnp.zeros((128 - n, 128), F32)], axis=0).T


def sorted_places(ids):
    hits = [ids == float(c + 1) for c in range(CL_DEV)]
    counted = dot(jnp.concatenate([onehot(h) for h in hits], axis=0), prefix_and_total())
    n = CL_DEV * 16
    below = onehot(
        lax.broadcasted_iota(jnp.int32, (n, n), 1) < lax.broadcasted_iota(jnp.int32, (n, n), 0)
    )
    offsets = dot(below, counted[:, 128:].astype(BF16))
    inside = counted[:, :128] + offsets
    place = jnp.full((16, 128), 4096.0, F32)
    starts = []
    for c in range(CL_DEV):
        place = jnp.where(hits[c], inside[16 * c : 16 * (c + 1)], place)
        starts.append(offsets[16 * c : 16 * c + 1])
    return place, starts


def kernel(
    q_ref, k_ref, v_ref, g_ref, id_ref, owner_ref, old_ref,
    o_ref, dq_ref, dk_ref, dv_ref, cent_ref,
    sbuf, rbuf, smeta, rmeta, xs, acc, res, sbuf2, rbuf2, final,
    fsend, frecv, msend, mrecv, bsend, brecv,
):
    me = lax.axis_index("seq")
    my_plane = me // PLANE
    my_place = lax.rem(me, PLANE)
    scale = 1.0 / math.sqrt(HD)

    barrier = pltpu.get_barrier_semaphore()

    def greet(i, carry):
        pl.semaphore_signal(
            barrier, inc=1, device_id={"seq": lax.rem(me + i, DEVS)}, device_id_type=MESH
        )
        return carry

    lax.fori_loop(1, DEVS, greet, 0)

    def remote(src, dst, send, recv, peer, slot):
        return pltpu.make_async_remote_copy(
            src_ref=src.at[peer], dst_ref=dst.at[slot], send_sem=send.at[peer],
            recv_sem=recv.at[slot], device_id={"seq": peer}, device_id_type=MESH,
        )

    def peer_at(k, j):
        return lax.rem(my_plane + k, PLANES) * PLANE + lax.rem(my_place + j, PLANE)

    def each_peer(k, step):
        def body(j, carry):
            step(peer_at(k, j))
            return carry

        lax.fori_loop(1 if k == 0 else 0, PLANE, body, 0)

    target, local, rank = token_slots(id_ref, owner_ref)
    slot = target * float(ROOM) + rank
    quarter = (lax.rem(me, 4) * ROOM).astype(F32)
    lane_of = onehot(iota((128, TOK), 0) == rank + quarter)
    labels = jnp.where(iota((DEVS, TOK), 0) == target, local + 1.0, 0.0).astype(BF16)
    smeta[...] = dot_nt(labels, lane_of).reshape(DEVS, 1, 128)

    rows = jnp.concatenate([q_ref[...], k_ref[...], v_ref[...], g_ref[...]], axis=1)

    def fill(p, carry):
        pick = onehot(iota((CHUNK, TOK), 0) + (p * CHUNK).astype(F32) == slot)
        block = dot(pick, rows).astype(BF16)
        sbuf[pl.ds(p * PLANE, PLANE)] = block.reshape(PLANE, ROOM, 4 * HD)
        return carry

    lax.fori_loop(0, PLANES, fill, 0)

    pl.semaphore_wait(barrier, DEVS - 1)
    for k in ORDER:
        each_peer(k, lambda d: remote(smeta, rmeta, msend, mrecv, d, me).start())
    for k in ORDER:
        each_peer(k, lambda d: remote(sbuf, rbuf, fsend, frecv, d, me).start())
    rbuf[me] = sbuf[me]
    rmeta[me] = smeta[me]

    acc[...] = jnp.zeros_like(acc)
    xs[pl.ds(0, 128)] = jnp.zeros((128, 4 * HD), BF16)
    for k in ORDER:
        each_peer(k, lambda d: remote(smeta, rmeta, msend, mrecv, d, d).wait_recv())
    ids = jnp.sum(rmeta[...].reshape(16, 4, 128), axis=1)
    place, starts = sorted_places(ids)
    place_cols = turned(place)
    place_ref_rows = place

    for k in ORDER:
        kb = (PLANES - k) % PLANES
        each_peer(kb, lambda d: remote(sbuf, rbuf, fsend, frecv, d, d).wait_recv())
        p = lax.rem(my_plane + kb, PLANES)
        chosen = iota((16, 128), 0)
        halves = []
        for h in range(2):
            row = jnp.sum(
                jnp.where(chosen == (2 * p + h).astype(F32), place_ref_rows, 0.0),
                axis=0, keepdims=True,
            )
            halves.append(iota((TOK, 128), 0) == row)
        pick = onehot(jnp.concatenate(halves, axis=1))
        block = rbuf[pl.ds(p * PLANE, PLANE)].reshape(CHUNK, 4 * HD)
        acc[...] += dot(pick, block)
    xs[pl.ds(128, TOK)] = acc[...].astype(BF16)

    at = iota((BLOCKS, 128), 0) * 128.0 + iota((BLOCKS, 128), 1)
    first = jnp.zeros((BLOCKS, 128), F32)
    for c in range(1, CL_DEV):
        first = jnp.where(at >= starts[c], starts[c], first)
    first_cols = turned(first)

    key_tail, value_tail = None, None
    for b in range(BLOCKS):
        mine = pl.ds(128 * (b + 1), 128)
        window = pl.ds(128 * b, 256)
        query = xs[mine, 0:HD]
        grad = xs[mine, 3 * HD : 4 * HD]
        keys = xs[window, HD : 2 * HD]
        vals = xs[window, 2 * HD : 3 * HD]
        scores = dot_nt(query, keys) * scale
        key_at = iota((128, 256), 1) + 128.0 * (b - 1)
        query_at = iota((128, 256), 0) + 128.0 * b
        allowed = (key_at <= query_at) & (key_at >= first_cols[:, b : b + 1])
        scores = jnp.where(allowed, scores, -1e30)
        weights = jnp.exp(scores - jnp.max(scores, axis=-1, keepdims=True))
        probs = weights / jnp.sum(weights, axis=-1, keepdims=True)
        probs_low = probs.astype(BF16)
        attn = dot(probs_low, vals).astype(BF16)
        delta = jnp.sum(grad.astype(F32) * attn.astype(F32), axis=-1, keepdims=True)
        dprobs = dot_nt(grad, vals)
        dscores = (probs * (dprobs - delta) * scale).astype(BF16)
        res[pl.ds(128 * b, 128), 0:HD] = attn
        res[pl.ds(128 * b, 128), HD : 2 * HD] = dot(dscores, keys).astype(BF16)
        dkeys = dot_tn(dscores, query)
        dvals = dot_tn(probs_low, grad)
        if b > 0:
            before = pl.ds(128 * (b - 1), 128)
            res[before, 2 * HD : 3 * HD] = (key_tail + dkeys[:128]).astype(BF16)
            res[before, 3 * HD : 4 * HD] = (value_tail + dvals[:128]).astype(BF16)
        key_tail, value_tail = dkeys[128:], dvals[128:]
    last = pl.ds(128 * (BLOCKS - 1), 128)
    res[last, 2 * HD : 3 * HD] = key_tail.astype(BF16)
    res[last, 3 * HD : 4 * HD] = value_tail.astype(BF16)

    results = res[...]
    for k in ORDER:
        p = lax.rem(my_plane + k, PLANES)
        chosen = iota((128, 128), 1)
        halves = []
        for h in range(2):
            col = jnp.sum(
                jnp.where(chosen == (2 * p + h).astype(F32), place_cols, 0.0),
                axis=1, keepdims=True,
            )
            halves.append(iota((128, TOK), 1) == col)
        pick = onehot(jnp.concatenate(halves, axis=0))
        block = dot(pick, results).astype(BF16)
        sbuf2[pl.ds(p * PLANE, PLANE)] = block.reshape(PLANE, ROOM, 4 * HD)
        each_peer(k, lambda d: remote(sbuf2, rbuf2, bsend, brecv, d, me).start())
    rbuf2[me] = sbuf2[me]

    start_rows = jnp.concatenate(starts, axis=0)
    end_rows = jnp.concatenate(starts[1:] + [jnp.full((1, 128), float(TOK), F32)], axis=0)
    sums = jnp.zeros((CL_DEV, HD), F32)
    for b in range(BLOCKS):
        row_at = iota((CL_DEV, 128), 1) + 128.0 * b
        owned = onehot((row_at >= start_rows) & (row_at < end_rows))
        sums = sums + dot(owned, xs[pl.ds(128 * (b + 1), 128), HD : 2 * HD])
    blended = 0.5 * old_ref[...] + 0.5 * sums / (end_rows - start_rows)
    power = jnp.mean(blended * blended, axis=-1, keepdims=True)
    cent_ref[...] = blended * lax.rsqrt(power + 1e-6)

    slot_cols = turned(jnp.concatenate([slot[:, 128 * b : 128 * (b + 1)] for b in range(8)], axis=0))
    slot_cols = [slot_cols[:, b : b + 1] for b in range(BLOCKS)]
    final[...] = jnp.zeros_like(final)
    for k in ORDER:
        kb = (PLANES - k) % PLANES
        each_peer(kb, lambda d: remote(sbuf2, rbuf2, bsend, brecv, d, d).wait_recv())
        p = lax.rem(my_plane + kb, PLANES)
        slot_at = iota((128, CHUNK), 1) + (p * CHUNK).astype(F32)
        pick = onehot(jnp.concatenate([slot_at == col for col in slot_cols], axis=0))
        block = rbuf2[pl.ds(p * PLANE, PLANE)].reshape(CHUNK, 4 * HD)
        final[...] += dot(pick, block)
    o_ref[...] = final[:, 0:HD].astype(BF16)
    dq_ref[...] = final[:, HD : 2 * HD].astype(BF16)
    dk_ref[...] = final[:, 2 * HD : 3 * HD].astype(BF16)
    dv_ref[...] = final[:, 3 * HD : 4 * HD].astype(BF16)

    for k in ORDER:
        each_peer(k, lambda d: remote(smeta, rmeta, msend, mrecv, d, me).wait_send())
        each_peer(k, lambda d: remote(sbuf, rbuf, fsend, frecv, d, me).wait_send())
        each_peer(k, lambda d: remote(sbuf2, rbuf2, bsend, brecv, d, me).wait_send())


def shards(queries, key_rows, values, out_grad, cluster_id, cluster_owner, old_centroids):
    vmem = pl.BlockSpec(memory_space=pltpu.VMEM)
    block = (DEVS, ROOM, 4 * HD)
    row_out = jax.ShapeDtypeStruct((TOK, HD), BF16)
    sems = pltpu.SemaphoreType.DMA((DEVS,))
    outs = pl.pallas_call(
        kernel,
        out_shape=(row_out, row_out, row_out, row_out, jax.ShapeDtypeStruct((CL_DEV, HD), F32)),
        in_specs=[vmem] * 7,
        out_specs=(vmem,) * 5,
        scratch_shapes=[
            pltpu.VMEM(block, BF16),
            pltpu.VMEM(block, BF16),
            pltpu.VMEM((DEVS, 1, 128), F32),
            pltpu.VMEM((DEVS, 1, 128), F32),
            pltpu.VMEM((TOK + 128, 4 * HD), BF16),
            pltpu.VMEM((TOK, 4 * HD), F32),
            pltpu.VMEM((TOK, 4 * HD), BF16),
            pltpu.VMEM(block, BF16),
            pltpu.VMEM(block, BF16),
            pltpu.VMEM((TOK, 4 * HD), F32),
            sems, sems, sems, sems, sems, sems,
        ],
        compiler_params=pltpu.CompilerParams(
            collective_id=0, has_side_effects=True, vmem_limit_bytes=56 << 20
        ),
    )(queries, key_rows, values, out_grad, cluster_id, cluster_owner, old_centroids[0])
    return outs[0], outs[1], outs[2], outs[3], outs[4][None]


def solution(mesh):
    return jax.shard_map(
        shards,
        mesh=mesh,
        in_specs=(
            P(("dp", "seq"), None),
            P(("dp", "seq"), None),
            P(("dp", "seq"), None),
            P(("dp", "seq"), None),
            P("dp", "seq"),
            P("dp", None),
            P("dp", "seq", None),
        ),
        out_specs=(
            P(("dp", "seq"), None),
            P(("dp", "seq"), None),
            P(("dp", "seq"), None),
            P(("dp", "seq"), None),
            P("dp", "seq", None),
        ),
        check_vma=False,
    )
```

time: 434 us -> 130 us (0.30)
  blocking collectives: 160 us -> 0 us
  Pallas kernels: 0 us -> 124 us
  local copies, waits for them, and re-layouts: 107 us -> 5.11 us
  waiting for transfers between devices: 61.5 us -> 0 us
  other arithmetic: 31.6 us -> 0 us
  starting transfers between devices: 30.7 us -> 0 us
  matrix products: 24.7 us -> 0 us
  between operations: 15.2 us -> 0.66 us
    unnamed x1 -> x0, blocking collectives: 160 us -> none
    pallas_call x0 -> x1, Pallas kernels: none -> 124 us  [shards(): pl.pallas_call(kernel, out_shape=(row_out, row_out, row_out, row_out, jax...]
    gather x15 -> x0, local copies, waits for them, and re-layouts: 99.3 us -> none  [the longest x12 88.6 us: take_rows(): return jnp.take(table, where, axis=0, mode='fill', fill_value=fill)]
    all_to_all x3 -> x0, waiting for transfers between devices: 33.5 us -> none  [the longest x1 33.5 us: shards(): lax.all_to_all(send_rows, 'seq', split_axis=1, concat_axis=1, tiled=True)]
    all_to_all x3 -> x0, starting transfers between devices: 30.6 us -> none  [the longest x1 13.2 us: shards(): lax.all_to_all(send_meta, 'seq', split_axis=1, concat_axis=1, tiled=True)]
    unnamed x2 -> x0, waiting for transfers between devices: 28 us -> none
    dot_general x115 -> x0, matrix products: 24.7 us -> none  [the longest x32 5.54 us: masked_scores(): jnp.einsum('hqd,hkd->hqk', query_c, key_c, preferred_element_type=jnp.flo...]
    dynamic_update_slice x16 -> x0, other arithmetic: 10.3 us -> none  [shards(): lax.map(backward_one, (rows_major, places_major, attn_major, peaks, totals))]
  transfers between devices with their start and end apart: 4 -> 0, of which waited for: 2 -> 0; matrix products, arithmetic and copies ran while one was open for 8% -> 0% of each run, Pallas kernels for 0% -> 0%
where the time goes in v1:
time: 130 us
  Pallas kernels  124 us (95%)
  local copies, waits for them, and re-layouts  5.11 us (4%)
    pallas_call x1, Pallas kernels, shards(): pl.pallas_call(kernel, out_shape=(row_out, row_out, row_out, row_out, jax...  124 us
    unnamed x13, local copies, waits for them, and re-layouts  5.11 us

profile of v1, /device:TPU:1, one launch (start us, length us, event | category | flops | bytes accessed | tf_op | source)
XLA Modules:
  0.0 130.1 jit_solution(11635229899134493795)
XLA Ops:
  0.6 124.4 %shard_map.110 = (bf16[1024,128]{1,0:T(8,128)(2,1)}, bf16[1024,128]{1,0:T(8,128)(2,1)}, bf16[1024,128]{1,0:T(8,128)(2,1)}, bf16[1024,128]{1,0:T(8,128)(2,1)}, f32[16,128]{1,0:T(8,128)}) custom-call(bf16[1024,128]{1,0:T(8,128)(2,1)} %q_ref.1, bf16[1024,128]{1,0:T(8,128)(2,1)} %k_ref.1, bf16[1024,128]{1,0:T(8,128)(2,1)} %v_ref.1, bf16[1024,128]{1,0:T(8,128)(2,1)} %g_ref.1, ...), custom_call_target="tpu_custom_call" | custom-call | tf_op jit(solution)/shard_map/pallas_call | solution.py:282
  125.0 0.0 copy-start.2
  125.0 1.7 %copy.17 = bf16[1024,128]{1,0:T(8,128)(2,1)} copy(bf16[1024,128]{1,0:T(8,128)(2,1)} %get-tuple-element.20) | data formatting | bytes 524288
  126.7 0.0 copy-done.2
  126.7 0.0 copy-start.1
  126.7 0.7 copy.18
  127.4 0.3 copy-done.1
  127.8 0.0 copy-start
  127.8 0.7 copy.19
  128.5 0.3 copy-done
  128.8 0.0 copy-start.3
  128.8 0.7 copy.20
  129.5 0.0 copy-done.3
  129.5 0.6 copy.21
Async XLA Ops:
  125.0 1.7 %copy-start.2 = (bf16[1024,128]{1,0:T(8,128)(2,1)S(1)}, bf16[1024,128]{1,0:T(8,128)(2,1)}, u32[]{:S(2)}) copy-start(bf16[1024,128]{1,0:T(8,128)(2,1)} %get-tuple-element.21) | copy-start | bytes 786436
  126.7 1.0 copy-start.1
  127.8 1.0 copy-start
  128.8 0.7 copy-start.3

commit v2 on v1

v2 whole, which is shorter than its diff:
```python
import functools
import math

import jax
import jax.numpy as jnp
from jax import lax
from jax.experimental import pallas as pl
from jax.experimental.pallas import tpu as pltpu
from jax.sharding import PartitionSpec as P

MESH = pl.DeviceIdType.MESH
HD = 128
CL_DEV = 16
TOK = 1024
DEVS = 64
ROOM = 32
PLANE = 8
PLANES = DEVS // PLANE
CHUNK = PLANE * ROOM
BLOCKS = TOK // 128
ORDER = (4, 1, 7, 3, 5, 2, 6, 0)
BF16 = jnp.bfloat16
F32 = jnp.float32


def dot(a, b):
    return jnp.dot(a, b, preferred_element_type=F32)


def dot_nt(a, b):
    return lax.dot_general(a, b, (((1,), (1,)), ((), ())), preferred_element_type=F32)


def dot_tn(a, b):
    return lax.dot_general(a, b, (((0,), (0,)), ((), ())), preferred_element_type=F32)


def iota(shape, dim):
    return lax.broadcasted_iota(jnp.int32, shape, dim).astype(F32)


def onehot(mask):
    return jnp.where(mask, 1.0, 0.0).astype(BF16)


def prefix_and_total():
    row = lax.broadcasted_iota(jnp.int32, (128, 256), 0)
    col = lax.broadcasted_iota(jnp.int32, (128, 256), 1)
    return onehot((row < col) | (col >= 128))


def token_slots(cluster_id, owner):
    ident = cluster_id[...]
    low = onehot(lax.broadcasted_iota(jnp.int32, (128, TOK), 0) == lax.rem(ident, 128))
    table = jnp.concatenate([owner[:, 128 * b : 128 * (b + 1)] for b in range(8)], axis=0)
    table_dev = lax.div(table, CL_DEV)
    table_loc = table - table_dev * CL_DEV
    tables = jnp.concatenate([table_dev, table_loc], axis=0).astype(F32).astype(BF16)
    found = dot(tables, low)
    high = lax.broadcasted_iota(jnp.int32, (8, TOK), 0) == lax.div(ident, 128)
    target = jnp.sum(jnp.where(high, found[:8], 0.0), axis=0, keepdims=True)
    local = jnp.sum(jnp.where(high, found[8:], 0.0), axis=0, keepdims=True)
    device = iota((DEVS, 128), 0)
    members = [device == target[:, 128 * b : 128 * (b + 1)] for b in range(BLOCKS)]
    counted = dot(jnp.concatenate([onehot(m) for m in members], axis=0), prefix_and_total())
    running = jnp.zeros((DEVS, 128), F32)
    ranks = []
    for b in range(BLOCKS):
        part = counted[DEVS * b : DEVS * (b + 1)]
        ranks.append(
            jnp.sum(jnp.where(members[b], part[:, :128] + running, 0.0), axis=0, keepdims=True)
        )
        running = running + part[:, 128:]
    rank = jnp.concatenate(ranks, axis=1)
    return target, local, rank


def turned(rows):
    n = rows.shape[0]
    return jnp.concatenate([rows, jnp.zeros((128 - n, 128), F32)], axis=0).T


def sorted_places(ids):
    hits = [ids == float(c + 1) for c in range(CL_DEV)]
    counted = dot(jnp.concatenate([onehot(h) for h in hits], axis=0), prefix_and_total())
    n = CL_DEV * 16
    below = onehot(
        lax.broadcasted_iota(jnp.int32, (n, n), 1) < lax.broadcasted_iota(jnp.int32, (n, n), 0)
    )
    offsets = dot(below, counted[:, 128:].astype(BF16))
    inside = counted[:, :128] + offsets
    place = jnp.full((16, 128), 4096.0, F32)
    starts = []
    for c in range(CL_DEV):
        place = jnp.where(hits[c], inside[16 * c : 16 * (c + 1)], place)
        starts.append(offsets[16 * c : 16 * c + 1])
    return place, starts


def plane_rows(place, p):
    at = lax.broadcasted_iota(jnp.int32, (16, 128), 0)
    return [
        jnp.sum(jnp.where(at == 2 * p + h, place, 0.0), axis=0, keepdims=True) for h in range(2)
    ]


def plane_cols(cols, p):
    at = lax.broadcasted_iota(jnp.int32, (128, 128), 1)
    return [jnp.sum(jnp.where(at == 2 * p + h, cols, 0.0), axis=1, keepdims=True) for h in range(2)]


def kernel(
    q_ref, k_ref, v_ref, g_ref, id_ref, owner_ref, old_ref,
    o_ref, dq_ref, dk_ref, dv_ref, cent_ref,
    smeta, rmeta, sqk, rqk, sv, rv, sg, rg, sa, ra, sd, rd,
    gather, ungather, final, xqk, xv, xg, acc, probs_ref, res,
    column_sem, send_sem, meta_sem, qk_sem, v_sem, g_sem, a_sem, d_sem,
):
    me = lax.axis_index("seq")
    my_plane = me // PLANE
    my_place = lax.rem(me, PLANE)
    scale = 1.0 / math.sqrt(HD)

    def peer_at(k, j):
        return lax.rem(my_plane + k, PLANES) * PLANE + lax.rem(my_place + j, PLANE)

    def signal(sem, k, j):
        pl.semaphore_signal(
            sem, inc=1, device_id={"seq": peer_at(k, j)}, device_id_type=MESH
        )

    barrier = pltpu.get_barrier_semaphore()
    for k in ORDER[:-1]:
        signal(barrier, k, 0)
    for j in range(1, PLANE):
        signal(barrier, 0, j)

    kinds = {
        "meta": (0, smeta, rmeta, meta_sem),
        "qk": (1, sqk, rqk, qk_sem),
        "v": (2, sv, rv, v_sem),
        "g": (3, sg, rg, g_sem),
        "a": (4, sa, ra, a_sem),
        "d": (5, sd, rd, d_sem),
    }

    def start(kind, k, first, last):
        index, src, dst, sem = kinds[kind]

        def body(j, carry):
            peer = peer_at(k, j)
            pltpu.make_async_remote_copy(
                src_ref=src.at[peer], dst_ref=dst.at[me], send_sem=send_sem.at[index],
                recv_sem=sem.at[my_plane], device_id={"seq": peer}, device_id_type=MESH,
            ).start()
            return carry

        lax.fori_loop(first, last, body, 0)

    def start_plane(kind, k):
        start(kind, k, 1 if k == 0 else 0, PLANE)

    def arrived(kind, k):
        _, _, dst, sem = kinds[kind]
        p = lax.rem(my_plane + k, PLANES)
        some = dst.at[pl.ds(p * PLANE, PLANE - 1 if k == 0 else PLANE)]
        pltpu.make_async_copy(some, some, sem.at[p]).wait()
        return p

    def sent(kind):
        index, src, _, _ = kinds[kind]
        some = src.at[pl.ds(0, DEVS - 1)]
        pltpu.make_async_copy(some, some, send_sem.at[index]).wait()

    def keep_own(kind):
        _, src, dst, _ = kinds[kind]
        dst[me] = src[me]

    def plane_of(ref, p):
        block = ref[pl.ds(p * PLANE, PLANE)]
        return block.reshape(CHUNK, block.shape[-1])

    def put_plane(ref, p, value):
        ref[pl.ds(p * PLANE, PLANE)] = value.astype(BF16).reshape(PLANE, ROOM, value.shape[-1])

    target, local, rank = token_slots(id_ref, owner_ref)
    slot = target * float(ROOM) + rank
    rows = jnp.concatenate([q_ref[...], k_ref[...], v_ref[...], g_ref[...]], axis=1)

    def fill(p, carry):
        pick = onehot(iota((CHUNK, TOK), 0) + (p * CHUNK).astype(F32) == slot)
        block = dot(pick, rows)
        put_plane(sqk, p, block[:, : 2 * HD])
        put_plane(sv, p, block[:, 2 * HD : 3 * HD])
        put_plane(sg, p, block[:, 3 * HD :])
        return carry

    lax.fori_loop(0, PLANES, fill, 0)

    quarter = (lax.rem(me, 4) * ROOM).astype(F32)
    lane_of = onehot(iota((128, TOK), 0) == rank + quarter)
    labels = jnp.where(iota((DEVS, TOK), 0) == target, local + 1.0, 0.0).astype(BF16)
    smeta[...] = dot_nt(labels, lane_of).reshape(DEVS, 1, 128)

    pl.semaphore_wait(barrier, 2 * PLANE - 2)
    for k in ORDER[:-1]:
        signal(column_sem, k, 0)
    for k in ORDER[:-1]:
        start("qk", k, 0, 1)
    pl.semaphore_wait(column_sem, PLANE - 1)
    for k in ORDER:
        start("qk", k, 1, PLANE)
    for kind in ("meta", "v", "g"):
        for k in ORDER:
            start_plane(kind, k)
    for kind in ("meta", "qk", "v", "g"):
        keep_own(kind)

    slot_cols = turned(jnp.concatenate([slot[:, 128 * b : 128 * (b + 1)] for b in range(8)], axis=0))
    slot_cols = [slot_cols[:, b : b + 1] for b in range(BLOCKS)]

    def build_final(p, carry):
        slot_at = iota((128, CHUNK), 1) + (p * CHUNK).astype(F32)
        final[p] = onehot(jnp.concatenate([slot_at == col for col in slot_cols], axis=0))
        return carry

    lax.fori_loop(0, PLANES, build_final, 0)

    for k in ORDER:
        arrived("meta", (PLANES - k) % PLANES)
    ids = jnp.sum(rmeta[...].reshape(16, 4, 128), axis=1)
    place, starts = sorted_places(ids)
    place_cols = turned(place)

    def build(p, carry):
        rows_of = plane_rows(place, p)
        gather[p] = onehot(jnp.concatenate([iota((TOK, 128), 0) == r for r in rows_of], axis=1))
        cols_of = plane_cols(place_cols, p)
        ungather[p] = onehot(jnp.concatenate([iota((128, TOK), 1) == c for c in cols_of], axis=0))
        return carry

    lax.fori_loop(0, PLANES, build, 0)

    at = iota((BLOCKS, 128), 0) * 128.0 + iota((BLOCKS, 128), 1)
    first = jnp.zeros((BLOCKS, 128), F32)
    for c in range(1, CL_DEV):
        first = jnp.where(at >= starts[c], starts[c], first)
    first_cols = turned(first)

    def collect(kind, matrix):
        _, _, dst, _ = kinds[kind]
        width = dst.shape[-1]
        for i, k in enumerate(ORDER):
            p = arrived(kind, (PLANES - k) % PLANES)
            part = dot(matrix[p], plane_of(dst, p))
            if i == PLANES - 1:
                return acc[:, :width] + part
            acc[:, :width] = part if i == 0 else acc[:, :width] + part

    front = pl.ds(0, 128)
    body = pl.ds(128, TOK)
    xqk[front] = jnp.zeros((128, 2 * HD), BF16)
    xv[front] = jnp.zeros((128, HD), BF16)

    xqk[body] = collect("qk", gather).astype(BF16)
    for b in range(BLOCKS):
        query = xqk[pl.ds(128 * (b + 1), 128), :HD]
        keys = xqk[pl.ds(128 * b, 256), HD:]
        scores = dot_nt(query, keys) * scale
        key_at = iota((128, 256), 1) + 128.0 * (b - 1)
        query_at = iota((128, 256), 0) + 128.0 * b
        allowed = (key_at <= query_at) & (key_at >= first_cols[:, b : b + 1])
        scores = jnp.where(allowed, scores, -1e30)
        weights = jnp.exp(scores - jnp.max(scores, axis=-1, keepdims=True))
        probs_ref[b] = weights / jnp.sum(weights, axis=-1, keepdims=True)

    start_rows = jnp.concatenate(starts, axis=0)
    end_rows = jnp.concatenate(starts[1:] + [jnp.full((1, 128), float(TOK), F32)], axis=0)
    sums = jnp.zeros((CL_DEV, HD), F32)
    for b in range(BLOCKS):
        row_at = iota((CL_DEV, 128), 1) + 128.0 * b
        owned = onehot((row_at >= start_rows) & (row_at < end_rows))
        sums = sums + dot(owned, xqk[pl.ds(128 * (b + 1), 128), HD:])
    blended = 0.5 * old_ref[...] + 0.5 * sums / (end_rows - start_rows)
    power = jnp.mean(blended * blended, axis=-1, keepdims=True)
    cent_ref[...] = blended * lax.rsqrt(power + 1e-6)

    xv[body] = collect("v", gather).astype(BF16)
    attn = [
        dot(probs_ref[b].astype(BF16), xv[pl.ds(128 * b, 256)]).astype(BF16) for b in range(BLOCKS)
    ]
    outs = jnp.concatenate(attn, axis=0)
    res[:, :HD] = outs
    for k in ORDER:
        p = lax.rem(my_plane + k, PLANES)
        put_plane(sa, p, dot(ungather[p], outs))
        start_plane("a", k)
    keep_own("a")

    xg[...] = collect("g", gather).astype(BF16)
    key_tail, value_tail = None, None
    for b in range(BLOCKS):
        mine = pl.ds(128 * b, 128)
        window = pl.ds(128 * b, 256)
        query = xqk[pl.ds(128 * (b + 1), 128), :HD]
        keys = xqk[window, HD:]
        grad = xg[mine]
        probs = probs_ref[b]
        delta = jnp.sum(
            grad.astype(F32) * res[mine, :HD].astype(F32), axis=-1, keepdims=True
        )
        dprobs = dot_nt(grad, xv[window])
        dscores = (probs * (dprobs - delta) * scale).astype(BF16)
        res[mine, HD : 2 * HD] = dot(dscores, keys).astype(BF16)
        dkeys = dot_tn(dscores, query)
        dvals = dot_tn(probs.astype(BF16), grad)
        if b > 0:
            before = pl.ds(128 * (b - 1), 128)
            res[before, 2 * HD : 3 * HD] = (key_tail + dkeys[:128]).astype(BF16)
            res[before, 3 * HD :] = (value_tail + dvals[:128]).astype(BF16)
        key_tail, value_tail = dkeys[128:], dvals[128:]
    last = pl.ds(128 * (BLOCKS - 1), 128)
    res[last, 2 * HD : 3 * HD] = key_tail.astype(BF16)
    res[last, 3 * HD :] = value_tail.astype(BF16)

    grads = res[:, HD:]
    for k in ORDER:
        p = lax.rem(my_plane + k, PLANES)
        put_plane(sd, p, dot(ungather[p], grads))
        start_plane("d", k)
    keep_own("d")
    for kind in ("meta", "qk", "v", "g"):
        sent(kind)

    o_ref[...] = collect("a", final).astype(BF16)
    sent("a")
    found = collect("d", final).astype(BF16)
    dq_ref[...] = found[:, :HD]
    dk_ref[...] = found[:, HD : 2 * HD]
    dv_ref[...] = found[:, 2 * HD :]
    sent("d")


def hand_over(*refs):
    n = len(refs) // 2
    for src, dst in zip(refs[:n], refs[n:]):
        dst[...] = src[...]


def shards(queries, key_rows, values, out_grad, cluster_id, cluster_owner, old_centroids):
    vmem = pl.BlockSpec(memory_space=pltpu.VMEM)
    anywhere = pl.BlockSpec(memory_space=pl.ANY)
    row_out = jax.ShapeDtypeStruct((TOK, HD), BF16)
    out_shape = (row_out, row_out, row_out, row_out, jax.ShapeDtypeStruct((CL_DEV, HD), F32))

    def pair(width):
        return [pltpu.VMEM((DEVS, ROOM, width), BF16)] * 2

    by_plane = pltpu.SemaphoreType.DMA((PLANES,))
    outs = pl.pallas_call(
        kernel,
        out_shape=out_shape,
        in_specs=[vmem] * 7,
        out_specs=(vmem,) * 5,
        scratch_shapes=[
            pltpu.VMEM((DEVS, 1, 128), F32),
            pltpu.VMEM((DEVS, 1, 128), F32),
            *pair(2 * HD), *pair(HD), *pair(HD), *pair(HD), *pair(3 * HD),
            pltpu.VMEM((PLANES, TOK, CHUNK), BF16),
            pltpu.VMEM((PLANES, CHUNK, TOK), BF16),
            pltpu.VMEM((PLANES, TOK, CHUNK), BF16),
            pltpu.VMEM((TOK + 128, 2 * HD), BF16),
            pltpu.VMEM((TOK + 128, HD), BF16),
            pltpu.VMEM((TOK, HD), BF16),
            pltpu.VMEM((TOK, 3 * HD), F32),
            pltpu.VMEM((BLOCKS, 128, 256), F32),
            pltpu.VMEM((TOK, 4 * HD), BF16),
            pltpu.SemaphoreType.REGULAR,
            pltpu.SemaphoreType.DMA((6,)),
            by_plane, by_plane, by_plane, by_plane, by_plane, by_plane,
        ],
        compiler_params=pltpu.CompilerParams(
            collective_id=0, has_side_effects=True, vmem_limit_bytes=56 << 20
        ),
    )(queries, key_rows, values, out_grad, cluster_id, cluster_owner, old_centroids[0])
    outs = pl.pallas_call(
        hand_over,
        out_shape=out_shape,
        in_specs=[vmem] * 5,
        out_specs=(vmem,) * 5,
    )(*outs)
    return outs[0], outs[1], outs[2], outs[3], outs[4][None]


def solution(mesh):
    return jax.shard_map(
        shards,
        mesh=mesh,
        in_specs=(
            P(("dp", "seq"), None),
            P(("dp", "seq"), None),
            P(("dp", "seq"), None),
            P(("dp", "seq"), None),
            P("dp", "seq"),
            P("dp", None),
            P("dp", "seq", None),
        ),
        out_specs=(
            P(("dp", "seq"), None),
            P(("dp", "seq"), None),
            P(("dp", "seq"), None),
            P(("dp", "seq"), None),
            P("dp", "seq", None),
        ),
        check_vma=False,
    )
```

time: 130 us -> 111 us (0.85)
  Pallas kernels: 124 us -> 110 us
  local copies, waits for them, and re-layouts: 5.11 us -> 0 us
    pallas_call x1 -> x2, Pallas kernels: 124 us -> 110 us  [the longest x1 108 us: shards(): pl.pallas_call(kernel, out_shape=out_shape, in_specs=[vmem] * 7, out_spec...]
    unnamed x13 -> x0, local copies, waits for them, and re-layouts: 5.11 us -> none
where the time goes in v2:
time: 111 us
  Pallas kernels  110 us (99%)
    pallas_call x1, Pallas kernels, shards(): pl.pallas_call(kernel, out_shape=out_shape, in_specs=[vmem] * 7, out_spec...  108 us

profile of v2, /device:TPU:1, one launch (start us, length us, event | category | flops | bytes accessed | tf_op | source)
XLA Modules:
  0.0 111.1 jit_solution(6461357561369092616)
XLA Ops:
  0.6 108.3 %shard_map.110 = (bf16[1024,128]{1,0:T(8,128)(2,1)}, bf16[1024,128]{1,0:T(8,128)(2,1)}, bf16[1024,128]{1,0:T(8,128)(2,1)}, bf16[1024,128]{1,0:T(8,128)(2,1)}, f32[16,128]{1,0:T(8,128)}) custom-call(bf16[1024,128]{1,0:T(8,128)(2,1)} %q_ref.1, bf16[1024,128]{1,0:T(8,128)(2,1)} %k_ref.1, bf16[1024,128]{1,0:T(8,128)(2,1)} %v_ref.1, bf16[1024,128]{1,0:T(8,128)(2,1)} %g_ref.1, ...), custom_call_target="tpu_custom_call" | custom-call | tf_op jit(solution)/shard_map/pallas_call | solution.py:360
  108.9 2.2 %shard_map.111 = (bf16[1024,128]{1,0:T(8,128)(2,1)}, bf16[1024,128]{1,0:T(8,128)(2,1)}, bf16[1024,128]{1,0:T(8,128)(2,1)}, bf16[1024,128]{1,0:T(8,128)(2,1)}, f32[16,128]{1,0:T(8,128)}) custom-call(bf16[1024,128]{1,0:T(8,128)(2,1)} %get-tuple-element.15.refs_0_, bf16[1024,128]{1,0:T(8,128)(2,1)} %get-tuple-element.16.refs_1_, ...), custom_call_target="tpu_custom_call" | custom-call | tf_op jit(solution)/shard_map/pallas_call | solution.py:386

commit v3 on v2

--- a/solution.py
+++ b/solution.py
@@ -19,6 +19,9 @@
 CHUNK = PLANE * ROOM
 BLOCKS = TOK // 128
 ORDER = (4, 1, 7, 3, 5, 2, 6, 0)
+SEATS = 24
+EXTRA = 16
+PARTS = 4
 BF16 = jnp.bfloat16
 F32 = jnp.float32
 
@@ -341,6 +344,461 @@
     sent("d")
 
 
+def seated_rank(seats, member):
+    n = seats
+    counted = dot(jnp.concatenate([onehot(m) for m in member], axis=0), prefix_and_total())
+    running = jnp.zeros((n, 128), F32)
+    ranks = []
+    for b in range(BLOCKS):
+        part = counted[n * b : n * (b + 1)]
+        ranks.append(
+            jnp.sum(jnp.where(member[b], part[:, :128] + running, 0.0), axis=0, keepdims=True)
+        )
+        running = running + part[:, 128:]
+    return jnp.concatenate(ranks, axis=1)
+
+
+def split_features(block, rows):
+    f = block.shape[1] // HD
+    return [block[:, HD * j : HD * (j + 1)].reshape(-1, rows, HD) for j in range(f)]
+
+
+def kernel_fast(
+    q_ref, k_ref, v_ref, g_ref, id_ref, owner_ref, old_ref,
+    o_ref, dq_ref, dk_ref, dv_ref, cent_ref, flag_ref,
+    smeta, rmeta, smx, rmx, sx, rx, sbuf, rbuf, sa, ra, sd, rd, sy, ry, sw, rw, sflag, rflag,
+    gather, ungather, final, xgather, xungather, wide, xqk, xv, xg, acc, probs_ref, res,
+    column_sem, send_sem, meta_sem, qk_sem, v_sem, g_sem, a_sem, d_sem, one_sem,
+):
+    me = lax.axis_index("seq")
+    my_part = lax.axis_index("dp")
+    my_plane = me // PLANE
+    my_place = lax.rem(me, PLANE)
+    scale = 1.0 / math.sqrt(HD)
+    UNIT = 65536.0
+    NONE = 8388608.0
+
+    def peer_at(k, j):
+        return lax.rem(my_plane + k, PLANES) * PLANE + lax.rem(my_place + j, PLANE)
+
+    def part_at(i):
+        return lax.rem(my_part + i, PARTS)
+
+    def signal(sem, k, j):
+        pl.semaphore_signal(sem, inc=1, device_id={"seq": peer_at(k, j)}, device_id_type=MESH)
+
+    barrier = pltpu.get_barrier_semaphore()
+    for k in ORDER[:-1]:
+        signal(barrier, k, 0)
+    for j in range(1, PLANE):
+        signal(barrier, 0, j)
+    for i in range(1, PARTS):
+        pl.semaphore_signal(barrier, inc=1, device_id={"dp": part_at(i)}, device_id_type=MESH)
+
+    kinds = {
+        "meta": (0, smeta, rmeta, meta_sem, 0, 1),
+        "qk": (1, sbuf, rbuf, qk_sem, 0, 2 * SEATS),
+        "v": (2, sbuf, rbuf, v_sem, 2 * SEATS, 32),
+        "g": (3, sbuf, rbuf, g_sem, 2 * SEATS + 32, 16),
+        "a": (4, sa, ra, a_sem, 0, 16),
+        "d": (5, sd, rd, d_sem, 0, 4 * SEATS - 16),
+    }
+
+    def start(kind, k, first, last):
+        index, src, dst, sem, low, count = kinds[kind]
+        some = pl.ds(low, count)
+
+        def body(j, carry):
+            peer = peer_at(k, j)
+            pltpu.make_async_remote_copy(
+                src_ref=src.at[peer, some], dst_ref=dst.at[me, some],
+                send_sem=send_sem.at[index], recv_sem=sem.at[my_plane],
+                device_id={"seq": peer}, device_id_type=MESH,
+            ).start()
+            return carry
+
+        lax.fori_loop(first, last, body, 0)
+
+    def start_plane(kind, k):
+        start(kind, k, 1 if k == 0 else 0, PLANE)
+
+    def arrived(kind, k):
+        _, _, dst, sem, low, count = kinds[kind]
+        p = lax.rem(my_plane + k, PLANES)
+        some = dst.at[pl.ds(p * PLANE, PLANE - 1 if k == 0 else PLANE), pl.ds(low, count)]
+        pltpu.make_async_copy(some, some, sem.at[p]).wait()
+        return p
+
+    def sent(kind):
+        index, src, _, _, low, count = kinds[kind]
+        some = src.at[pl.ds(0, DEVS - 1), pl.ds(low, count)]
+        pltpu.make_async_copy(some, some, send_sem.at[index]).wait()
+
+    ones = {
+        "x": (6, sx, rx.at[my_place], 0),
+        "mx": (7, smx, rmx.at[my_place], 1),
+        "fx": (8, rx, rx, 2),
+        "fm": (9, rmx, rmx, 3),
+        "y": (10, sy, ry, 4),
+        "w": (11, sw, rw, 5),
+        "flag": (12, sflag, rflag, 6),
+    }
+
+    def column(kind):
+        index, src, dst, sem = ones[kind]
+        for k in ORDER[:-1]:
+            p = lax.rem(my_plane + k, PLANES)
+            pltpu.make_async_remote_copy(
+                src_ref=src.at[p], dst_ref=dst.at[my_plane], send_sem=send_sem.at[index],
+                recv_sem=one_sem.at[sem], device_id={"seq": peer_at(k, 0)}, device_id_type=MESH,
+            ).start()
+
+    def across(kind, forward, first=0, last=PLANES):
+        index, src, dst, sem = ones[kind]
+        some = pl.ds(first, last - first)
+        for j in range(1, PLANE):
+            seat = lax.rem(my_place + j, PLANE)
+            pltpu.make_async_remote_copy(
+                src_ref=src.at[my_place if forward else seat, some],
+                dst_ref=dst.at[my_place, some],
+                send_sem=send_sem.at[index], recv_sem=one_sem.at[sem],
+                device_id={"seq": peer_at(0, j)}, device_id_type=MESH,
+            ).start()
+
+    def one_wait(kind, n, sending):
+        index, src, dst, sem = ones[kind]
+        some = (src if sending else dst).at[pl.ds(0, n)]
+        pltpu.make_async_copy(
+            some, some, send_sem.at[index] if sending else one_sem.at[sem]
+        ).wait()
+
+    target, local, rank = token_slots(id_ref, owner_ref)
+    plane_row = jnp.floor(target * (1.0 / PLANE))
+    seat_row = target - plane_row * float(PLANE)
+    direct = rank < float(SEATS)
+    slot = jnp.where(direct, target * float(SEATS) + rank, -1.0)
+    member = [
+        (iota((PLANES, 128), 0) == plane_row[:, 128 * b : 128 * (b + 1)])
+        & (rank[:, 128 * b : 128 * (b + 1)] >= float(SEATS))
+        for b in range(BLOCKS)
+    ]
+    extra = seated_rank(PLANES, member)
+    fits = (rank >= float(SEATS)) & (extra < float(EXTRA))
+    xslot = jnp.where(fits, plane_row * float(EXTRA) + extra, -1.0)
+    lost = jnp.max(jnp.where(extra >= float(EXTRA), 1.0, 0.0), axis=1, keepdims=True)
+
+    rows = jnp.concatenate([q_ref[...], k_ref[...], v_ref[...], g_ref[...]], axis=1)
+    block = dot(onehot(iota((PLANES * EXTRA, TOK), 0) == xslot), rows)
+    sx[...] = jnp.concatenate(split_features(block, EXTRA), axis=1).astype(BF16)
+
+    def fill(p, carry):
+        pick = onehot(iota((PLANE * SEATS, TOK), 0) + (p * PLANE * SEATS).astype(F32) == slot)
+        parts = split_features(dot(pick, rows), SEATS)
+        sbuf[pl.ds(p * PLANE, PLANE)] = jnp.concatenate(parts, axis=1).astype(BF16)
+        return carry
+
+    lax.fori_loop(0, PLANES, fill, 0)
+
+    when = iota((1, TOK), 1)
+    when_high = jnp.floor(when * (1.0 / 32))
+    when_low = when - 32.0 * when_high
+    here = (me * TOK).astype(F32)
+
+    def keys_of(rows_at, label, lanes_at):
+        n = rows_at.shape[0]
+        stack = [jnp.where(rows_at, r, 0.0) for r in (label, when_high, when_low)]
+        found = dot_nt(jnp.concatenate(stack, axis=0).astype(BF16), onehot(lanes_at))
+        label = found[:n]
+        key = label * UNIT + 32.0 * found[n : 2 * n] + found[2 * n :]
+        return key + jnp.where(label > 0.0, here, 0.0)
+
+    lane = jnp.where(direct, rank + (my_place * SEATS).astype(F32), -1.0)
+    key = keys_of(iota((DEVS, TOK), 0) == target, local + 1.0, iota((256, TOK), 0) == lane)
+    key = jnp.where(iota((DEVS, 256), 1) == 255.0, lost, key)
+    smeta[...] = key.reshape(DEVS, 1, 256)
+    lane = jnp.where(fits, extra + (my_plane * EXTRA).astype(F32), -1.0)
+    label = local + 1.0 + seat_row * float(CL_DEV)
+    key = keys_of(iota((PLANES, TOK), 0) == plane_row, label, iota((128, TOK), 0) == lane)
+    smx[...] = key.reshape(PLANES, 1, 128)
+
+    pl.semaphore_wait(barrier, 2 * PLANE - 2 + PARTS - 1)
+    for k in ORDER[:-1]:
+        signal(column_sem, k, 0)
+    column("x")
+    column("mx")
+    rx[my_place, my_plane] = sx[my_plane]
+    rmx[my_place, my_plane] = smx[my_plane]
+    for k in ORDER[:-1]:
+        start("qk", k, 0, 1)
+    pl.semaphore_wait(column_sem, PLANE - 1)
+    for k in ORDER:
+        start_plane("meta", k)
+    for k in ORDER[:3]:
+        start("qk", k, 1, PLANE)
+    rbuf[me] = sbuf[me]
+    rmeta[me] = smeta[me]
+    one_wait("x", PLANES - 1, False)
+    one_wait("mx", PLANES - 1, False)
+    across("fm", True)
+    for k, first, last in zip(ORDER[3:], (0, 2, 4, 6, 7), (2, 4, 6, 7, 8)):
+        start("qk", k, 1, PLANE)
+        across("fx", True, first, last)
+    for kind in ("v", "g"):
+        for k in ORDER:
+            start_plane(kind, k)
+
+    slot_cols = turned(jnp.concatenate([slot[:, 128 * b : 128 * (b + 1)] for b in range(8)], axis=0))
+    slot_cols = [slot_cols[:, b : b + 1] for b in range(BLOCKS)]
+
+    def build_final(p, carry):
+        slot_at = iota((128, 256), 1) + (p * PLANE * SEATS).astype(F32)
+        final[p] = onehot(jnp.concatenate([slot_at == col for col in slot_cols], axis=0))
+        return carry
+
+    lax.fori_loop(0, PLANES, build_final, 0)
+
+    for k in ORDER:
+        arrived("meta", (PLANES - k) % PLANES)
+    got = jnp.sum(rmeta[...].reshape(PLANES, PLANE, 256), axis=1)
+    lost_any = jnp.max(got[:, 255:256], axis=0, keepdims=True)
+    sflag[0] = jnp.broadcast_to(lost_any, (1, 128))
+    for i in range(1, PARTS):
+        pltpu.make_async_remote_copy(
+            src_ref=sflag.at[0], dst_ref=rflag.at[my_part], send_sem=send_sem.at[12],
+            recv_sem=one_sem.at[6], device_id={"dp": part_at(i)}, device_id_type=MESH,
+        ).start()
+    rflag[my_part] = sflag[0]
+
+    one_wait("fm", PLANE - 1, False)
+    got_extra = jnp.sum(rmx[...].reshape(PLANE, PLANES, 128), axis=1)
+    base = (my_place * CL_DEV).astype(F32) * UNIT
+    got_extra = got_extra - base
+    mine = (got_extra >= UNIT) & (got_extra < (1.0 + CL_DEV) * UNIT)
+    got_extra = jnp.where(mine, got_extra, 0.0)
+    tail = jnp.where(iota((PLANES, 128), 1) < 64.0, got[:, 128:], 0.0)
+    keys_all = jnp.concatenate([got[:, :128], tail, got_extra], axis=0)
+    keys_all = jnp.where(keys_all < UNIT, NONE, keys_all)
+    key_cols = turned(keys_all)
+    n_rows = 3 * PLANES
+    for r in range(n_rows):
+        wide[r] = jnp.broadcast_to(key_cols[:, r : r + 1], (128, 128))
+
+    def count(r, sums):
+        less = wide[r]
+        out = []
+        for c in range(n_rows):
+            hit = jnp.where(less < keys_all[c : c + 1], 1.0, 0.0)
+            out.append(sums[c] + jnp.sum(hit.reshape(16, 8, 128), axis=0))
+        return tuple(out)
+
+    zero = jnp.zeros((8, 128), F32)
+    counts = lax.fori_loop(0, n_rows, count, (zero,) * n_rows)
+    place = jnp.concatenate([jnp.sum(c, axis=0, keepdims=True) for c in counts], axis=0)
+    place = jnp.where(keys_all == NONE, 4096.0, place)
+    place_cols = turned(place)
+    starts = [jnp.zeros((1, 128), F32)]
+    for c in range(1, CL_DEV):
+        below = jnp.where(keys_all < (1.0 + c) * UNIT, 1.0, 0.0)
+        below = jnp.sum(jnp.sum(below, axis=0, keepdims=True), axis=1, keepdims=True)
+        starts.append(jnp.broadcast_to(below, (1, 128)))
+
+    def build(p, carry):
+        at = lax.broadcasted_iota(jnp.int32, (n_rows, 128), 0)
+        first, second = (
+            jnp.sum(jnp.where(at == p + PLANES * h, place, 0.0), axis=0, keepdims=True)
+            for h in range(2)
+        )
+        gather[p] = onehot(
+            jnp.concatenate(
+                [iota((TOK, 128), 0) == first, iota((TOK, 128), 0) == second], axis=1
+            )
+        )
+        at = lax.broadcasted_iota(jnp.int32, (128, 128), 1)
+        first, second = (
+            jnp.sum(jnp.where(at == p + PLANES * h, place_cols, 0.0), axis=1, keepdims=True)
+            for h in range(2)
+        )
+        ungather[p, 0:128] = onehot(iota((128, TOK), 1) == first)
+        ungather[p, 128:192] = onehot(iota((64, TOK), 1) == second[:64])
+        return carry
+
+    lax.fori_loop(0, PLANES, build, 0)
+    for u in range(PLANE):
+        r = 2 * PLANES + u
+        xgather[:, 128 * u : 128 * (u + 1)] = onehot(iota((TOK, 128), 0) == place[r : r + 1])
+        xungather[128 * u : 128 * (u + 1)] = onehot(iota((128, TOK), 1) == place_cols[:, r : r + 1])
+
+    at = iota((BLOCKS, 128), 0) * 128.0 + iota((BLOCKS, 128), 1)
+    first = jnp.zeros((BLOCKS, 128), F32)
+    for c in range(1, CL_DEV):
+        first = jnp.where(at >= starts[c], starts[c], first)
+    first_cols = turned(first)
+
+    def together(parts):
+        return jnp.concatenate([p.reshape(-1, HD) for p in parts], axis=1).astype(BF16)
+
+    def extras(ref, features):
+        return jnp.concatenate(
+            [
+                ref[:, :, EXTRA * f : EXTRA * (f + 1)].reshape(PLANE * PLANES * EXTRA, HD)
+                for f in features
+            ],
+            axis=1,
+        )
+
+    def collect(kind, features, cut):
+        width = HD * len(features)
+        acc[:, :width] = dot(xgather[...], extras(rx, features))
+        for k in ORDER:
+            p = arrived(kind, (PLANES - k) % PLANES)
+            part = dot(gather[p, :, : PLANE * SEATS], together(cut(pl.ds(p * PLANE, PLANE))))
+            if k == ORDER[-1]:
+                return acc[:, :width] + part
+            acc[:, :width] += part
+
+    def cut_qk(at):
+        block = rbuf[at, 0 : 2 * SEATS].astype(F32)
+        return [block[:, :SEATS], block[:, SEATS:]]
+
+    def cut_v(at):
+        return [rbuf[at, 2 * SEATS : 2 * SEATS + 32].astype(F32)[:, :SEATS]]
+
+    def cut_g(at):
+        return [rbuf[at, 4 * SEATS - 32 : 4 * SEATS].astype(F32)[:, 32 - SEATS :]]
+
+    front = pl.ds(0, 128)
+    body = pl.ds(128, TOK)
+    xqk[front] = jnp.zeros((128, 2 * HD), BF16)
+    xv[front] = jnp.zeros((128, HD), BF16)
+
+    one_wait("fx", PLANE - 1, False)
+    xqk[body] = collect("qk", (0, 1), cut_qk).astype(BF16)
+    for b in range(BLOCKS):
+        query = xqk[pl.ds(128 * (b + 1), 128), :HD]
+        keys = xqk[pl.ds(128 * b, 256), HD:]
+        scores = dot_nt(query, keys) * scale
+        key_at = iota((128, 256), 1) + 128.0 * (b - 1)
+        query_at = iota((128, 256), 0) + 128.0 * b
+        allowed = (key_at <= query_at) & (key_at >= first_cols[:, b : b + 1])
+        scores = jnp.where(allowed, scores, -1e30)
+        weights = jnp.exp(scores - jnp.max(scores, axis=-1, keepdims=True))
+        probs_ref[b] = weights / jnp.sum(weights, axis=-1, keepdims=True)
+
+    start_rows = jnp.concatenate(starts, axis=0)
+    end_rows = jnp.concatenate(starts[1:] + [jnp.full((1, 128), float(TOK), F32)], axis=0)
+    sums = jnp.zeros((CL_DEV, HD), F32)
+    for b in range(BLOCKS):
+        row_at = iota((CL_DEV, 128), 1) + 128.0 * b
+        owned = onehot((row_at >= start_rows) & (row_at < end_rows))
+        sums = sums + dot(owned, xqk[pl.ds(128 * (b + 1), 128), HD:])
+    blended = 0.5 * old_ref[...] + 0.5 * sums / (end_rows - start_rows)
+    power = jnp.mean(blended * blended, axis=-1, keepdims=True)
+    cent_ref[...] = blended * lax.rsqrt(power + 1e-6)
+
+    xv[body] = collect("v", (2,), cut_v).astype(BF16)
+    attn = [
+        dot(probs_ref[b].astype(BF16), xv[pl.ds(128 * b, 256)]).astype(BF16) for b in range(BLOCKS)
+    ]
+    outs = jnp.concatenate(attn, axis=0)
+    res[:, :HD] = outs
+    for k in ORDER:
+        p = lax.rem(my_plane + k, PLANES)
+        block = dot(ungather[p], outs).reshape(PLANE, SEATS, HD)
+        sa[pl.ds(p * PLANE, PLANE)] = block[:, :16].astype(BF16)
+        start_plane("a", k)
+    ra[me] = sa[me]
+
+    xg[...] = collect("g", (3,), cut_g).astype(BF16)
+    key_tail, value_tail = None, None
+    for b in range(BLOCKS):
+        mine = pl.ds(128 * b, 128)
+        window = pl.ds(128 * b, 256)
+        query = xqk[pl.ds(128 * (b + 1), 128), :HD]
+        keys = xqk[window, HD:]
+        grad = xg[mine]
+        probs = probs_ref[b]
+        delta = jnp.sum(grad.astype(F32) * res[mine, :HD].astype(F32), axis=-1, keepdims=True)
+        dprobs = dot_nt(grad, xv[window])
+        dscores = (probs * (dprobs - delta) * scale).astype(BF16)
+        res[mine, HD : 2 * HD] = dot(dscores, keys).astype(BF16)
+        dkeys = dot_tn(dscores, query)
+        dvals = dot_tn(probs.astype(BF16), grad)
+        if b > 0:
+            before = pl.ds(128 * (b - 1), 128)
+            res[before, 2 * HD : 3 * HD] = (key_tail + dkeys[:128]).astype(BF16)
+            res[before, 3 * HD :] = (value_tail + dvals[:128]).astype(BF16)
+        key_tail, value_tail = dkeys[128:], dvals[128:]
+    last = pl.ds(128 * (BLOCKS - 1), 128)
+    res[last, 2 * HD : 3 * HD] = key_tail.astype(BF16)
+    res[last, 3 * HD :] = value_tail.astype(BF16)
+
+    results = res[...]
+    back = dot(xungather[...], results)
+    back = [
+        back[:, HD * f : HD * (f + 1)].reshape(PLANE, PLANES, EXTRA, HD).astype(BF16)
+        for f in range(4)
+    ]
+    sy[...] = jnp.concatenate(back, axis=2)
+    ry[my_place] = sy[my_place]
+    for i, k in enumerate(ORDER):
+        p = lax.rem(my_plane + k, PLANES)
+        parts = split_features(dot(ungather[p], results), SEATS)
+        parts[0] = parts[0][:, 16:]
+        sd[pl.ds(p * PLANE, PLANE)] = jnp.concatenate(parts, axis=1).astype(BF16)
+        start_plane("d", k)
+        if i < 4:
+            across("y", False, 2 * i, 2 * i + 2)
+    rd[me] = sd[me]
+    one_wait("y", PLANE - 1, False)
+    sw[...] = jnp.sum(ry[...].astype(F32), axis=0).astype(BF16)
+    column("w")
+    rw[my_plane] = sw[my_plane]
+
+    for kind in ("meta", "qk", "v", "g", "a"):
+        sent(kind)
+    for kind, n in (("x", 7), ("mx", 7), ("fx", 7), ("fm", 7), ("y", 7)):
+        one_wait(kind, n, True)
+
+    one_wait("flag", PARTS - 1, False)
+    flag_ref[...] = jnp.max(rflag[...], axis=0)
+    one_wait("flag", PARTS - 1, True)
+
+    def cut_back(at):
+        head = ra[at].astype(F32)
+        rest = rd[at].astype(F32)
+        cuts = [rest[:, SEATS * f - 16 : SEATS * (f + 1) - 16] for f in range(1, 4)]
+        return [jnp.concatenate([head, rest[:, : SEATS - 16]], axis=1)] + cuts
+
+    for k in ORDER:
+        arrived("a", (PLANES - k) % PLANES)
+    for k in ORDER:
+        p = arrived("d", (PLANES - k) % PLANES)
+        part = dot(final[p, :, : PLANE * SEATS], together(cut_back(pl.ds(p * PLANE, PLANE))))
+        if k == ORDER[0]:
+            acc[...] = part
+        else:
+            acc[...] += part
+    xslot_cols = turned(
+        jnp.concatenate([xslot[:, 128 * b : 128 * (b + 1)] for b in range(8)], axis=0)
+    )
+    pick = onehot(
+        jnp.concatenate(
+            [iota((128, 128), 1) == xslot_cols[:, b : b + 1] for b in range(BLOCKS)], axis=0
+        )
+    )
+    one_wait("w", PLANES - 1, False)
+    late = jnp.concatenate(
+        [rw[:, EXTRA * f : EXTRA * (f + 1)].reshape(PLANES * EXTRA, HD) for f in range(4)], axis=1
+    )
+    found = (acc[...] + dot(pick, late)).astype(BF16)
+    o_ref[...] = found[:, :HD]
+    dq_ref[...] = found[:, HD : 2 * HD]
+    dk_ref[...] = found[:, 2 * HD : 3 * HD]
+    dv_ref[...] = found[:, 3 * HD :]
+    sent("d")
+    one_wait("w", 7, True)
+
+
 def hand_over(*refs):
     n = len(refs) // 2
     for src, dst in zip(refs[:n], refs[n:]):
@@ -349,45 +807,89 @@
 
 def shards(queries, key_rows, values, out_grad, cluster_id, cluster_owner, old_centroids):
     vmem = pl.BlockSpec(memory_space=pltpu.VMEM)
-    anywhere = pl.BlockSpec(memory_space=pl.ANY)
     row_out = jax.ShapeDtypeStruct((TOK, HD), BF16)
     out_shape = (row_out, row_out, row_out, row_out, jax.ShapeDtypeStruct((CL_DEV, HD), F32))
-
-    def pair(width):
-        return [pltpu.VMEM((DEVS, ROOM, width), BF16)] * 2
-
-    by_plane = pltpu.SemaphoreType.DMA((PLANES,))
+    by_plane = [pltpu.SemaphoreType.DMA((PLANES,))] * 6
+    args = (queries, key_rows, values, out_grad, cluster_id, cluster_owner, old_centroids[0])
+
+    def pair(rows, width, n=DEVS, dtype=BF16):
+        return [pltpu.VMEM((n, rows, width), dtype)] * 2
+
+    def params(ident):
+        return pltpu.CompilerParams(
+            collective_id=ident, has_side_effects=True, vmem_limit_bytes=56 << 20
+        )
+
+    sorted_rows = [
+        pltpu.VMEM((TOK + 128, 2 * HD), BF16),
+        pltpu.VMEM((TOK + 128, HD), BF16),
+        pltpu.VMEM((TOK, HD), BF16),
+    ]
+    work = [
+        pltpu.VMEM((BLOCKS, 128, 256), F32),
+        pltpu.VMEM((TOK, 4 * HD), BF16),
+        pltpu.SemaphoreType.REGULAR,
+    ]
+
+    def general(*args):
+        return pl.pallas_call(
+            kernel,
+            out_shape=out_shape,
+            in_specs=[vmem] * 7,
+            out_specs=(vmem,) * 5,
+            scratch_shapes=[
+                *pair(1, 128, dtype=F32),
+                *pair(ROOM, 2 * HD), *pair(ROOM, HD), *pair(ROOM, HD),
+                *pair(ROOM, HD), *pair(ROOM, 3 * HD),
+                pltpu.VMEM((PLANES, TOK, CHUNK), BF16),
+                pltpu.VMEM((PLANES, CHUNK, TOK), BF16),
+                pltpu.VMEM((PLANES, TOK, CHUNK), BF16),
+                *sorted_rows,
+                pltpu.VMEM((TOK, 3 * HD), F32),
+                *work,
+                pltpu.SemaphoreType.DMA((6,)),
+                *by_plane,
+            ],
+            compiler_params=params(1),
+        )(*args)
+
+    extra_rows = pltpu.VMEM((PLANE, PLANES, 4 * EXTRA, HD), BF16)
+    *outs, flag = pl.pallas_call(
+        kernel_fast,
+        out_shape=out_shape + (jax.ShapeDtypeStruct((1, 128), F32),),
+        in_specs=[vmem] * 7,
+        out_specs=(vmem,) * 6,
+        scratch_shapes=[
+            *pair(1, 256, dtype=F32),
+            pltpu.VMEM((PLANES, 1, 128), F32),
+            pltpu.VMEM((PLANE, PLANES, 1, 128), F32),
+            pltpu.VMEM((PLANES, 4 * EXTRA, HD), BF16),
+            extra_rows,
+            *pair(4 * SEATS, HD), *pair(16, HD), *pair(4 * SEATS - 16, HD),
+            extra_rows, extra_rows,
+            *pair(4 * EXTRA, HD, PLANES),
+            *pair(1, 128, PARTS, F32),
+            pltpu.VMEM((PLANES, TOK, 256), BF16),
+            pltpu.VMEM((PLANES, PLANE * SEATS, TOK), BF16),
+            pltpu.VMEM((PLANES, TOK, 256), BF16),
+            pltpu.VMEM((TOK, TOK), BF16),
+            pltpu.VMEM((TOK, TOK), BF16),
+            pltpu.VMEM((3 * PLANES, 128, 128), F32),
+            *sorted_rows,
+            pltpu.VMEM((TOK, 4 * HD), F32),
+            *work,
+            pltpu.SemaphoreType.DMA((13,)),
+            *by_plane,
+            pltpu.SemaphoreType.DMA((7,)),
+        ],
+        compiler_params=params(0),
+    )(*args)
+
+    outs = lax.cond(
+        flag[0, 0] > 0.0, lambda args, outs: general(*args), lambda args, outs: outs, args, tuple(outs)
+    )
     outs = pl.pallas_call(
-        kernel,
-        out_shape=out_shape,
-        in_specs=[vmem] * 7,
-        out_specs=(vmem,) * 5,
-        scratch_shapes=[
-            pltpu.VMEM((DEVS, 1, 128), F32),
-            pltpu.VMEM((DEVS, 1, 128), F32),
-            *pair(2 * HD), *pair(HD), *pair(HD), *pair(HD), *pair(3 * HD),
-            pltpu.VMEM((PLANES, TOK, CHUNK), BF16),
-            pltpu.VMEM((PLANES, CHUNK, TOK), BF16),
-            pltpu.VMEM((PLANES, TOK, CHUNK), BF16),
-            pltpu.VMEM((TOK + 128, 2 * HD), BF16),
-            pltpu.VMEM((TOK + 128, HD), BF16),
-            pltpu.VMEM((TOK, HD), BF16),
-            pltpu.VMEM((TOK, 3 * HD), F32),
-            pltpu.VMEM((BLOCKS, 128, 256), F32),
-            pltpu.VMEM((TOK, 4 * HD), BF16),
-            pltpu.SemaphoreType.REGULAR,
-            pltpu.SemaphoreType.DMA((6,)),
-            by_plane, by_plane, by_plane, by_plane, by_plane, by_plane,
-        ],
-        compiler_params=pltpu.CompilerParams(
-            collective_id=0, has_side_effects=True, vmem_limit_bytes=56 << 20
-        ),
-    )(queries, key_rows, values, out_grad, cluster_id, cluster_owner, old_centroids[0])
-    outs = pl.pallas_call(
-        hand_over,
-        out_shape=out_shape,
-        in_specs=[vmem] * 5,
-        out_specs=(vmem,) * 5,
+        hand_over, out_shape=out_shape, in_specs=[vmem] * 5, out_specs=(vmem,) * 5
     )(*outs)
     return outs[0], outs[1], outs[2], outs[3], outs[4][None]
 

time: 111 us -> 102 us (0.919)
  Pallas kernels: 110 us -> 99.9 us
    pallas_call x1, Pallas kernels: 108 us -> 98.8 us  [shards(): pl.pallas_call(kernel_fast, out_shape=out_shape + (jax.ShapeDtypeStruct((...]
    pallas_call x1, Pallas kernels: 2.17 us -> 1.03 us  [shards(): pl.pallas_call(hand_over, out_shape=out_shape, in_specs=[vmem] * 5, out_s...]
where the time goes in v3:
time: 102 us
  Pallas kernels  99.9 us (98%)
    pallas_call x1, Pallas kernels, shards(): pl.pallas_call(kernel_fast, out_shape=out_shape + (jax.ShapeDtypeStruct((...  98.8 us

profile of v3, /device:TPU:1, one launch (start us, length us, event | category | flops | bytes accessed | tf_op | source)
XLA Modules:
  0.0 101.6 jit_solution(13647564238507972245)
XLA Ops:
  0.6 0.0 copy-start
  0.6 0.0 copy-start.1
  0.7 0.0 copy-start.2
  0.7 0.0 copy-start.3
  0.7 0.0 copy-start.6
  0.7 98.8 %shard_map.110 = (bf16[1024,128]{1,0:T(8,128)(2,1)S(1)}, bf16[1024,128]{1,0:T(8,128)(2,1)S(1)}, bf16[1024,128]{1,0:T(8,128)(2,1)S(1)}, bf16[1024,128]{1,0:T(8,12...) custom-call(bf16[1024,128]{1,0:T(8,128)(2,1)} %q_ref.1, bf16[1024,128]{1,0:T(8,128)(2,1)} %k_ref.1, ...), custom_call_target="tpu_custom_call" | custom-call | tf_op jit(solution)/shard_map/pallas_call | solution.py:857
  99.5 0.0 copy-start.4
  99.5 0.0 copy-start.7
  99.5 0.0 copy-start.5
  99.6 0.6 copy-done.7
  100.2 0.0 copy-done
  100.2 0.0 copy-done.1
  100.2 0.0 copy-done.2
  100.2 0.0 copy-done.3
  100.2 0.0 copy-done.6
  100.3 0.0 copy-done.4
  100.3 0.0 copy-done.5
  100.3 0.3 conditional.1
  100.5 1.0 %shard_map.111 = (bf16[1024,128]{1,0:T(8,128)(2,1)}, bf16[1024,128]{1,0:T(8,128)(2,1)}, bf16[1024,128]{1,0:T(8,128)(2,1)}, bf16[1024,128]{1,0:T(8,128)(2,1)}, f32[16,128]{1,0:T(8,128)}) custom-call(bf16[1024,128]{1,0:T(8,128)(2,1)S(1)} %get-tuple-element.58.refs_0_, bf16[1024,128]{1,0:T(8,128)(2,1)S(1)} %get-tuple-element.59.refs_1_, ...), custom_call_target="tpu_custom_call" | custom-call | tf_op jit(solution)/shard_map/pallas_call | solution.py:891
Async XLA Ops:
  0.6 99.6 %copy-start = (bf16[1024,128]{1,0:T(8,128)(2,1)S(1)}, bf16[1024,128]{1,0:T(8,128)(2,1)}, u32[]{:S(2)}) copy-start(bf16[1024,128]{1,0:T(8,128)(2,1)} %q_ref.1) | copy-start | bytes 786436
  0.6 99.6 %copy-start.1 = (bf16[1024,128]{1,0:T(8,128)(2,1)S(1)}, bf16[1024,128]{1,0:T(8,128)(2,1)}, u32[]{:S(2)}) copy-start(bf16[1024,128]{1,0:T(8,128)(2,1)} %k_ref.1) | copy-start | bytes 786436
  0.7 99.6 %copy-start.2 = (bf16[1024,128]{1,0:T(8,128)(2,1)S(1)}, bf16[1024,128]{1,0:T(8,128)(2,1)}, u32[]{:S(2)}) copy-start(bf16[1024,128]{1,0:T(8,128)(2,1)} %v_ref.1) | copy-start | bytes 786436
  0.7 99.6 %copy-start.3 = (bf16[1024,128]{1,0:T(8,128)(2,1)S(1)}, bf16[1024,128]{1,0:T(8,128)(2,1)}, u32[]{:S(2)}) copy-start(bf16[1024,128]{1,0:T(8,128)(2,1)} %g_ref.1) | copy-start | bytes 786436
  0.7 99.6 %copy-start.6 = (s32[1,1024]{1,0:T(1,128)S(1)}, s32[1,1024]{1,0:T(1,128)}, u32[]{:S(2)}) copy-start(s32[1,1024]{1,0:T(1,128)} %owner_ref.1) | copy-start | bytes 12292
  99.5 0.7 copy-start.4
  99.5 0.6 copy-start.7
  99.5 0.7 copy-start.5

commit v4 on v3

--- a/solution.py
+++ b/solution.py
@@ -20,7 +20,7 @@
 BLOCKS = TOK // 128
 ORDER = (4, 1, 7, 3, 5, 2, 6, 0)
 SEATS = 24
-EXTRA = 16
+EXTRA = 8
 PARTS = 4
 BF16 = jnp.bfloat16
 F32 = jnp.float32
@@ -488,16 +488,25 @@
     lost = jnp.max(jnp.where(extra >= float(EXTRA), 1.0, 0.0), axis=1, keepdims=True)
 
     rows = jnp.concatenate([q_ref[...], k_ref[...], v_ref[...], g_ref[...]], axis=1)
-    block = dot(onehot(iota((PLANES * EXTRA, TOK), 0) == xslot), rows)
-    sx[...] = jnp.concatenate(split_features(block, EXTRA), axis=1).astype(BF16)
-
-    def fill(p, carry):
+
+    def fill(k):
+        p = lax.rem(my_plane + k, PLANES)
         pick = onehot(iota((PLANE * SEATS, TOK), 0) + (p * PLANE * SEATS).astype(F32) == slot)
         parts = split_features(dot(pick, rows), SEATS)
         sbuf[pl.ds(p * PLANE, PLANE)] = jnp.concatenate(parts, axis=1).astype(BF16)
-        return carry
-
-    lax.fori_loop(0, PLANES, fill, 0)
+
+    fill(ORDER[0])
+    pl.semaphore_wait(barrier, 2 * PLANE - 2 + PARTS - 1)
+    for k in ORDER[:-1]:
+        signal(column_sem, k, 0)
+    for i, k in enumerate(ORDER[:-1]):
+        for kind in ("qk", "v", "g"):
+            start(kind, k, 0, 1)
+        fill(ORDER[i + 1])
+    block = dot(onehot(iota((PLANES * EXTRA, TOK), 0) == xslot), rows)
+    sx[...] = jnp.concatenate(split_features(block, EXTRA), axis=1).astype(BF16)
+    column("x")
+    rx[my_place, my_plane] = sx[my_plane]
 
     when = iota((1, TOK), 1)
     when_high = jnp.floor(when * (1.0 / 32))
@@ -516,20 +525,14 @@
     key = keys_of(iota((DEVS, TOK), 0) == target, local + 1.0, iota((256, TOK), 0) == lane)
     key = jnp.where(iota((DEVS, 256), 1) == 255.0, lost, key)
     smeta[...] = key.reshape(DEVS, 1, 256)
-    lane = jnp.where(fits, extra + (my_plane * EXTRA).astype(F32), -1.0)
+    first_lane = my_plane * EXTRA + lax.rem(my_place, 2) * 64
+    lane = jnp.where(fits, extra + first_lane.astype(F32), -1.0)
     label = local + 1.0 + seat_row * float(CL_DEV)
     key = keys_of(iota((PLANES, TOK), 0) == plane_row, label, iota((128, TOK), 0) == lane)
     smx[...] = key.reshape(PLANES, 1, 128)
 
-    pl.semaphore_wait(barrier, 2 * PLANE - 2 + PARTS - 1)
-    for k in ORDER[:-1]:
-        signal(column_sem, k, 0)
-    column("x")
     column("mx")
-    rx[my_place, my_plane] = sx[my_plane]
     rmx[my_place, my_plane] = smx[my_plane]
-    for k in ORDER[:-1]:
-        start("qk", k, 0, 1)
     pl.semaphore_wait(column_sem, PLANE - 1)
     for k in ORDER:
         start_plane("meta", k)
@@ -545,7 +548,7 @@
         across("fx", True, first, last)
     for kind in ("v", "g"):
         for k in ORDER:
-            start_plane(kind, k)
+            start(kind, k, 1, PLANE)
 
     slot_cols = turned(jnp.concatenate([slot[:, 128 * b : 128 * (b + 1)] for b in range(8)], axis=0))
     slot_cols = [slot_cols[:, b : b + 1] for b in range(BLOCKS)]
@@ -575,11 +578,12 @@
     got_extra = got_extra - base
     mine = (got_extra >= UNIT) & (got_extra < (1.0 + CL_DEV) * UNIT)
     got_extra = jnp.where(mine, got_extra, 0.0)
+    got_extra = jnp.sum(got_extra.reshape(PLANE // 2, 2, 128), axis=1)
     tail = jnp.where(iota((PLANES, 128), 1) < 64.0, got[:, 128:], 0.0)
     keys_all = jnp.concatenate([got[:, :128], tail, got_extra], axis=0)
     keys_all = jnp.where(keys_all < UNIT, NONE, keys_all)
     key_cols = turned(keys_all)
-    n_rows = 3 * PLANES
+    n_rows = 2 * PLANES + PLANE // 2
     for r in range(n_rows):
         wide[r] = jnp.broadcast_to(key_cols[:, r : r + 1], (128, 128))
 
@@ -623,7 +627,7 @@
         return carry
 
     lax.fori_loop(0, PLANES, build, 0)
-    for u in range(PLANE):
+    for u in range(PLANE // 2):
         r = 2 * PLANES + u
         xgather[:, 128 * u : 128 * (u + 1)] = onehot(iota((TOK, 128), 0) == place[r : r + 1])
         xungather[128 * u : 128 * (u + 1)] = onehot(iota((128, TOK), 1) == place_cols[:, r : r + 1])
@@ -638,13 +642,10 @@
         return jnp.concatenate([p.reshape(-1, HD) for p in parts], axis=1).astype(BF16)
 
     def extras(ref, features):
-        return jnp.concatenate(
-            [
-                ref[:, :, EXTRA * f : EXTRA * (f + 1)].reshape(PLANE * PLANES * EXTRA, HD)
-                for f in features
-            ],
-            axis=1,
-        )
+        low = EXTRA * features[0] // 16 * 16
+        block = ref[:, :, low : max(low + 16, EXTRA * (features[-1] + 1))].astype(F32)
+        cuts = [block[:, :, EXTRA * f - low : EXTRA * (f + 1) - low] for f in features]
+        return together(cuts)
 
     def collect(kind, features, cut):
         width = HD * len(features)
@@ -733,21 +734,21 @@
     res[last, 3 * HD :] = value_tail.astype(BF16)
 
     results = res[...]
-    back = dot(xungather[...], results)
-    back = [
-        back[:, HD * f : HD * (f + 1)].reshape(PLANE, PLANES, EXTRA, HD).astype(BF16)
-        for f in range(4)
-    ]
-    sy[...] = jnp.concatenate(back, axis=2)
-    ry[my_place] = sy[my_place]
     for i, k in enumerate(ORDER):
+        if i == 2:
+            back = dot(xungather[...], results)
+            back = [
+                back[:, HD * f : HD * (f + 1)].reshape(PLANE, PLANES, EXTRA, HD) for f in range(4)
+            ]
+            sy[...] = jnp.concatenate(back, axis=2).astype(BF16)
+            ry[my_place] = sy[my_place]
         p = lax.rem(my_plane + k, PLANES)
         parts = split_features(dot(ungather[p], results), SEATS)
         parts[0] = parts[0][:, 16:]
         sd[pl.ds(p * PLANE, PLANE)] = jnp.concatenate(parts, axis=1).astype(BF16)
         start_plane("d", k)
-        if i < 4:
-            across("y", False, 2 * i, 2 * i + 2)
+        if 2 <= i < 6:
+            across("y", False, 2 * i - 4, 2 * i - 2)
     rd[me] = sd[me]
     one_wait("y", PLANE - 1, False)
     sw[...] = jnp.sum(ry[...].astype(F32), axis=0).astype(BF16)
@@ -783,13 +784,13 @@
     )
     pick = onehot(
         jnp.concatenate(
-            [iota((128, 128), 1) == xslot_cols[:, b : b + 1] for b in range(BLOCKS)], axis=0
+            [iota((128, PLANES * EXTRA), 1) == xslot_cols[:, b : b + 1] for b in range(BLOCKS)],
+            axis=0,
         )
     )
     one_wait("w", PLANES - 1, False)
-    late = jnp.concatenate(
-        [rw[:, EXTRA * f : EXTRA * (f + 1)].reshape(PLANES * EXTRA, HD) for f in range(4)], axis=1
-    )
+    block = rw[...].astype(F32)
+    late = together([block[:, EXTRA * f : EXTRA * (f + 1)] for f in range(4)])
     found = (acc[...] + dot(pick, late)).astype(BF16)
     o_ref[...] = found[:, :HD]
     dq_ref[...] = found[:, HD : 2 * HD]
@@ -872,9 +873,9 @@
             pltpu.VMEM((PLANES, TOK, 256), BF16),
             pltpu.VMEM((PLANES, PLANE * SEATS, TOK), BF16),
             pltpu.VMEM((PLANES, TOK, 256), BF16),
-            pltpu.VMEM((TOK, TOK), BF16),
-            pltpu.VMEM((TOK, TOK), BF16),
-            pltpu.VMEM((3 * PLANES, 128, 128), F32),
+            pltpu.VMEM((TOK, DEVS * EXTRA), BF16),
+            pltpu.VMEM((DEVS * EXTRA, TOK), BF16),
+            pltpu.VMEM((2 * PLANES + PLANE // 2, 128, 128), F32),
             *sorted_rows,
             pltpu.VMEM((TOK, 4 * HD), F32),
             *work,

time: 102 us -> 95.1 us (0.932)
  Pallas kernels: 99.9 us -> 93.2 us
    pallas_call x1, Pallas kernels: 98.8 us -> 92.2 us  [shards(): pl.pallas_call(kernel_fast, out_shape=out_shape + (jax.ShapeDtypeStruct((...]
where the time goes in v4:
time: 95.1 us; the launch traced here: 95 us
  Pallas kernels  93.2 us (98%)
    pallas_call x1, Pallas kernels, shards(): pl.pallas_call(kernel_fast, out_shape=out_shape + (jax.ShapeDtypeStruct((...  92.2 us

profile of v4, /device:TPU:1, one launch (start us, length us, event | category | flops | bytes accessed | tf_op | source)
XLA Modules:
  0.0 95.0 jit_solution(14090611610294608541)
XLA Ops:
  0.6 0.0 copy-start
  0.6 0.0 copy-start.1
  0.7 0.0 copy-start.2
  0.7 0.0 copy-start.3
  0.7 0.0 copy-start.6
  0.7 92.2 %shard_map.110 = (bf16[1024,128]{1,0:T(8,128)(2,1)S(1)}, bf16[1024,128]{1,0:T(8,128)(2,1)S(1)}, bf16[1024,128]{1,0:T(8,128)(2,1)S(1)}, bf16[1024,128]{1,0:T(8,12...) custom-call(bf16[1024,128]{1,0:T(8,128)(2,1)} %q_ref.1, bf16[1024,128]{1,0:T(8,128)(2,1)} %k_ref.1, ...), custom_call_target="tpu_custom_call" | custom-call | tf_op jit(solution)/shard_map/pallas_call | solution.py:858
  92.9 0.0 copy-start.4
  92.9 0.0 copy-start.7
  92.9 0.0 copy-start.5
  92.9 0.6 copy-done.7
  93.5 0.0 copy-done
  93.6 0.0 copy-done.1
  93.6 0.0 copy-done.2
  93.6 0.0 copy-done.3
  93.6 0.0 copy-done.6
  93.6 0.0 copy-done.4
  93.6 0.0 copy-done.5
  93.6 0.3 conditional.1
  93.9 1.0 %shard_map.111 = (bf16[1024,128]{1,0:T(8,128)(2,1)}, bf16[1024,128]{1,0:T(8,128)(2,1)}, bf16[1024,128]{1,0:T(8,128)(2,1)}, bf16[1024,128]{1,0:T(8,128)(2,1)}, f32[16,128]{1,0:T(8,128)}) custom-call(bf16[1024,128]{1,0:T(8,128)(2,1)S(1)} %get-tuple-element.58.refs_0_, bf16[1024,128]{1,0:T(8,128)(2,1)S(1)} %get-tuple-element.59.refs_1_, ...), custom_call_target="tpu_custom_call" | custom-call | tf_op jit(solution)/shard_map/pallas_call | solution.py:892
Async XLA Ops:
  0.6 92.9 %copy-start = (bf16[1024,128]{1,0:T(8,128)(2,1)S(1)}, bf16[1024,128]{1,0:T(8,128)(2,1)}, u32[]{:S(2)}) copy-start(bf16[1024,128]{1,0:T(8,128)(2,1)} %q_ref.1) | copy-start | bytes 786436
  0.6 92.9 %copy-start.1 = (bf16[1024,128]{1,0:T(8,128)(2,1)S(1)}, bf16[1024,128]{1,0:T(8,128)(2,1)}, u32[]{:S(2)}) copy-start(bf16[1024,128]{1,0:T(8,128)(2,1)} %k_ref.1) | copy-start | bytes 786436
  0.7 92.9 %copy-start.2 = (bf16[1024,128]{1,0:T(8,128)(2,1)S(1)}, bf16[1024,128]{1,0:T(8,128)(2,1)}, u32[]{:S(2)}) copy-start(bf16[1024,128]{1,0:T(8,128)(2,1)} %v_ref.1) | copy-start | bytes 786436
  0.7 92.9 %copy-start.3 = (bf16[1024,128]{1,0:T(8,128)(2,1)S(1)}, bf16[1024,128]{1,0:T(8,128)(2,1)}, u32[]{:S(2)}) copy-start(bf16[1024,128]{1,0:T(8,128)(2,1)} %g_ref.1) | copy-start | bytes 786436
  0.7 92.9 %copy-start.6 = (s32[1,1024]{1,0:T(1,128)S(1)}, s32[1,1024]{1,0:T(1,128)}, u32[]{:S(2)}) copy-start(s32[1,1024]{1,0:T(1,128)} %owner_ref.1) | copy-start | bytes 12292
  92.9 0.7 copy-start.4
  92.9 0.6 copy-start.7
  92.9 0.7 copy-start.5

commit v5 on v4

--- a/solution.py
+++ b/solution.py
@@ -18,7 +18,7 @@
 PLANES = DEVS // PLANE
 CHUNK = PLANE * ROOM
 BLOCKS = TOK // 128
-ORDER = (4, 1, 7, 3, 5, 2, 6, 0)
+ORDER = (4, 3, 5, 2, 6, 1, 7, 0)
 SEATS = 24
 EXTRA = 8
 PARTS = 4
@@ -366,9 +366,9 @@
 def kernel_fast(
     q_ref, k_ref, v_ref, g_ref, id_ref, owner_ref, old_ref,
     o_ref, dq_ref, dk_ref, dv_ref, cent_ref, flag_ref,
-    smeta, rmeta, smx, rmx, sx, rx, sbuf, rbuf, sa, ra, sd, rd, sy, ry, sw, rw, sflag, rflag,
+    rows_in, load_sem, smeta, rmeta, smx, rmx, sx, rx, sbuf, rbuf, sa, ra, sc, rc, sd, rd, sy, ry, sw, rw, sflag, rflag,
     gather, ungather, final, xgather, xungather, wide, xqk, xv, xg, acc, probs_ref, res,
-    column_sem, send_sem, meta_sem, qk_sem, v_sem, g_sem, a_sem, d_sem, one_sem,
+    column_sem, send_sem, meta_sem, qk_sem, v_sem, g_sem, a_sem, c_sem, d_sem, one_sem,
 ):
     me = lax.axis_index("seq")
     my_part = lax.axis_index("dp")
@@ -387,6 +387,12 @@
     def signal(sem, k, j):
         pl.semaphore_signal(sem, inc=1, device_id={"seq": peer_at(k, j)}, device_id_type=MESH)
 
+    loads = [
+        pltpu.make_async_copy(ref, rows_in.at[:, pl.ds(HD * f, HD)], load_sem.at[f])
+        for f, ref in enumerate((q_ref, k_ref, v_ref, g_ref))
+    ]
+    for load in loads:
+        load.start()
     barrier = pltpu.get_barrier_semaphore()
     for k in ORDER[:-1]:
         signal(barrier, k, 0)
@@ -401,7 +407,8 @@
         "v": (2, sbuf, rbuf, v_sem, 2 * SEATS, 32),
         "g": (3, sbuf, rbuf, g_sem, 2 * SEATS + 32, 16),
         "a": (4, sa, ra, a_sem, 0, 16),
-        "d": (5, sd, rd, d_sem, 0, 4 * SEATS - 16),
+        "c": (13, sc, rc, c_sem, 0, 2 * SEATS - 16),
+        "d": (5, sd, rd, d_sem, 0, 2 * SEATS),
     }
 
     def start(kind, k, first, last):
@@ -487,7 +494,9 @@
     xslot = jnp.where(fits, plane_row * float(EXTRA) + extra, -1.0)
     lost = jnp.max(jnp.where(extra >= float(EXTRA), 1.0, 0.0), axis=1, keepdims=True)
 
-    rows = jnp.concatenate([q_ref[...], k_ref[...], v_ref[...], g_ref[...]], axis=1)
+    for load in loads:
+        load.wait()
+    rows = rows_in[...]
 
     def fill(k):
         p = lax.rem(my_plane + k, PLANES)
@@ -710,7 +719,25 @@
     ra[me] = sa[me]
 
     xg[...] = collect("g", (3,), cut_g).astype(BF16)
-    key_tail, value_tail = None, None
+    value_tail = None
+    for b in range(BLOCKS):
+        dvals = dot_tn(probs_ref[b].astype(BF16), xg[pl.ds(128 * b, 128)])
+        if b > 0:
+            res[pl.ds(128 * (b - 1), 128), 3 * HD :] = (value_tail + dvals[:128]).astype(BF16)
+        value_tail = dvals[128:]
+    res[pl.ds(128 * (BLOCKS - 1), 128), 3 * HD :] = value_tail.astype(BF16)
+
+    for k in ORDER:
+        p = lax.rem(my_plane + k, PLANES)
+        parts = [
+            dot(ungather[p], res[:, at]).reshape(PLANE, SEATS, HD)
+            for at in (slice(0, HD), slice(3 * HD, 4 * HD))
+        ]
+        block = jnp.concatenate([parts[0][:, 16:], parts[1]], axis=1).astype(BF16)
+        sc[pl.ds(p * PLANE, PLANE)] = block
+        start_plane("c", k)
+
+    key_tail = None
     for b in range(BLOCKS):
         mine = pl.ds(128 * b, 128)
         window = pl.ds(128 * b, 256)
@@ -723,39 +750,36 @@
         dscores = (probs * (dprobs - delta) * scale).astype(BF16)
         res[mine, HD : 2 * HD] = dot(dscores, keys).astype(BF16)
         dkeys = dot_tn(dscores, query)
-        dvals = dot_tn(probs.astype(BF16), grad)
         if b > 0:
             before = pl.ds(128 * (b - 1), 128)
             res[before, 2 * HD : 3 * HD] = (key_tail + dkeys[:128]).astype(BF16)
-            res[before, 3 * HD :] = (value_tail + dvals[:128]).astype(BF16)
-        key_tail, value_tail = dkeys[128:], dvals[128:]
+        key_tail = dkeys[128:]
     last = pl.ds(128 * (BLOCKS - 1), 128)
     res[last, 2 * HD : 3 * HD] = key_tail.astype(BF16)
-    res[last, 3 * HD :] = value_tail.astype(BF16)
-
-    results = res[...]
+
     for i, k in enumerate(ORDER):
         if i == 2:
-            back = dot(xungather[...], results)
+            back = dot(xungather[...], res[...])
             back = [
                 back[:, HD * f : HD * (f + 1)].reshape(PLANE, PLANES, EXTRA, HD) for f in range(4)
             ]
             sy[...] = jnp.concatenate(back, axis=2).astype(BF16)
             ry[my_place] = sy[my_place]
         p = lax.rem(my_plane + k, PLANES)
-        parts = split_features(dot(ungather[p], results), SEATS)
-        parts[0] = parts[0][:, 16:]
-        sd[pl.ds(p * PLANE, PLANE)] = jnp.concatenate(parts, axis=1).astype(BF16)
+        parts = split_features(dot(ungather[p], res[:, HD : 3 * HD]), SEATS)
+        block = jnp.concatenate(parts, axis=1).astype(BF16)
+        sd[pl.ds(p * PLANE, PLANE)] = block
         start_plane("d", k)
         if 2 <= i < 6:
             across("y", False, 2 * i - 4, 2 * i - 2)
+    rc[me] = sc[me]
     rd[me] = sd[me]
     one_wait("y", PLANE - 1, False)
     sw[...] = jnp.sum(ry[...].astype(F32), axis=0).astype(BF16)
     column("w")
     rw[my_plane] = sw[my_plane]
 
-    for kind in ("meta", "qk", "v", "g", "a"):
+    for kind in ("meta", "qk", "v", "g", "a", "c"):
         sent(kind)
     for kind, n in (("x", 7), ("mx", 7), ("fx", 7), ("fm", 7), ("y", 7)):
         one_wait(kind, n, True)
@@ -766,12 +790,14 @@
 
     def cut_back(at):
         head = ra[at].astype(F32)
-        rest = rd[at].astype(F32)
-        cuts = [rest[:, SEATS * f - 16 : SEATS * (f + 1) - 16] for f in range(1, 4)]
-        return [jnp.concatenate([head, rest[:, : SEATS - 16]], axis=1)] + cuts
-
-    for k in ORDER:
-        arrived("a", (PLANES - k) % PLANES)
+        rest = rc[at].astype(F32)
+        keys = rd[at].astype(F32)
+        outs = jnp.concatenate([head, rest[:, : SEATS - 16]], axis=1)
+        return [outs, keys[:, :SEATS], keys[:, SEATS:], rest[:, SEATS - 16 :]]
+
+    for kind in ("a", "c"):
+        for k in ORDER:
+            arrived(kind, (PLANES - k) % PLANES)
     for k in ORDER:
         p = arrived("d", (PLANES - k) % PLANES)
         part = dot(final[p, :, : PLANE * SEATS], together(cut_back(pl.ds(p * PLANE, PLANE))))
@@ -810,7 +836,7 @@
     vmem = pl.BlockSpec(memory_space=pltpu.VMEM)
     row_out = jax.ShapeDtypeStruct((TOK, HD), BF16)
     out_shape = (row_out, row_out, row_out, row_out, jax.ShapeDtypeStruct((CL_DEV, HD), F32))
-    by_plane = [pltpu.SemaphoreType.DMA((PLANES,))] * 6
+    by_plane = [pltpu.SemaphoreType.DMA((PLANES,))] * 7
     args = (queries, key_rows, values, out_grad, cluster_id, cluster_owner, old_centroids[0])
 
     def pair(rows, width, n=DEVS, dtype=BF16):
@@ -849,7 +875,7 @@
                 pltpu.VMEM((TOK, 3 * HD), F32),
                 *work,
                 pltpu.SemaphoreType.DMA((6,)),
-                *by_plane,
+                *by_plane[:6],
             ],
             compiler_params=params(1),
         )(*args)
@@ -858,15 +884,18 @@
     *outs, flag = pl.pallas_call(
         kernel_fast,
         out_shape=out_shape + (jax.ShapeDtypeStruct((1, 128), F32),),
-        in_specs=[vmem] * 7,
+        in_specs=[pl.BlockSpec(memory_space=pl.ANY)] * 4 + [vmem] * 3,
         out_specs=(vmem,) * 6,
         scratch_shapes=[
+            pltpu.VMEM((TOK, 4 * HD), BF16),
+            pltpu.SemaphoreType.DMA((4,)),
             *pair(1, 256, dtype=F32),
             pltpu.VMEM((PLANES, 1, 128), F32),
             pltpu.VMEM((PLANE, PLANES, 1, 128), F32),
             pltpu.VMEM((PLANES, 4 * EXTRA, HD), BF16),
             extra_rows,
-            *pair(4 * SEATS, HD), *pair(16, HD), *pair(4 * SEATS - 16, HD),
+            *pair(4 * SEATS, HD), *pair(16, HD),
+            *pair(2 * SEATS - 16, HD), *pair(2 * SEATS, HD),
             extra_rows, extra_rows,
             *pair(4 * EXTRA, HD, PLANES),
             *pair(1, 128, PARTS, F32),
@@ -879,7 +908,7 @@
             *sorted_rows,
             pltpu.VMEM((TOK, 4 * HD), F32),
             *work,
-            pltpu.SemaphoreType.DMA((13,)),
+            pltpu.SemaphoreType.DMA((14,)),
             *by_plane,
             pltpu.SemaphoreType.DMA((7,)),
         ],

time: 95.1 us -> 91.2 us (0.959)
  Pallas kernels: 93.2 us -> 89.2 us
    pallas_call x1, Pallas kernels: 92.2 us -> 88.2 us  [shards(): pl.pallas_call(kernel_fast, out_shape=out_shape + (jax.ShapeDtypeStruct((...]
where the time goes in v5:
time: 91.2 us; the launch traced here: 91 us
  Pallas kernels  89.2 us (98%)
    pallas_call x1, Pallas kernels, shards(): pl.pallas_call(kernel_fast, out_shape=out_shape + (jax.ShapeDtypeStruct((...  88.2 us

profile of v5, /device:TPU:1, one launch (start us, length us, event | category | flops | bytes accessed | tf_op | source)
XLA Modules:
  0.0 91.0 jit_solution(5697393659504212417)
XLA Ops:
  0.6 0.0 copy-start
  0.6 0.0 copy-start.1
  0.7 0.0 copy-start.2
  0.7 0.0 copy-start.3
  0.7 0.0 copy-start.6
  0.7 88.2 %shard_map.110 = (bf16[1024,128]{1,0:T(8,128)(2,1)S(1)}, bf16[1024,128]{1,0:T(8,128)(2,1)S(1)}, bf16[1024,128]{1,0:T(8,128)(2,1)S(1)}, bf16[1024,128]{1,0:T(8,12...) custom-call(bf16[1024,128]{1,0:T(8,128)(2,1)} %q_ref.1, bf16[1024,128]{1,0:T(8,128)(2,1)} %k_ref.1, ...), custom_call_target="tpu_custom_call" | custom-call | tf_op jit(solution)/shard_map/pallas_call | solution.py:884
  88.9 0.0 copy-start.4
  88.9 0.0 copy-start.7
  88.9 0.0 copy-start.5
  88.9 0.6 copy-done.7
  89.5 0.0 copy-done
  89.5 0.0 copy-done.1
  89.6 0.0 copy-done.2
  89.6 0.0 copy-done.3
  89.6 0.0 copy-done.6
  89.6 0.0 copy-done.4
  89.6 0.0 copy-done.5
  89.6 0.3 conditional.1
  89.9 1.0 %shard_map.111 = (bf16[1024,128]{1,0:T(8,128)(2,1)}, bf16[1024,128]{1,0:T(8,128)(2,1)}, bf16[1024,128]{1,0:T(8,128)(2,1)}, bf16[1024,128]{1,0:T(8,128)(2,1)}, f32[16,128]{1,0:T(8,128)}) custom-call(bf16[1024,128]{1,0:T(8,128)(2,1)S(1)} %get-tuple-element.58.refs_0_, bf16[1024,128]{1,0:T(8,128)(2,1)S(1)} %get-tuple-element.59.refs_1_, ...), custom_call_target="tpu_custom_call" | custom-call | tf_op jit(solution)/shard_map/pallas_call | solution.py:921
Async XLA Ops:
  0.6 88.9 %copy-start = (bf16[1024,128]{1,0:T(8,128)(2,1)S(1)}, bf16[1024,128]{1,0:T(8,128)(2,1)}, u32[]{:S(2)}) copy-start(bf16[1024,128]{1,0:T(8,128)(2,1)} %q_ref.1) | copy-start | bytes 786436
  0.6 88.9 %copy-start.1 = (bf16[1024,128]{1,0:T(8,128)(2,1)S(1)}, bf16[1024,128]{1,0:T(8,128)(2,1)}, u32[]{:S(2)}) copy-start(bf16[1024,128]{1,0:T(8,128)(2,1)} %k_ref.1) | copy-start | bytes 786436
  0.7 88.9 %copy-start.2 = (bf16[1024,128]{1,0:T(8,128)(2,1)S(1)}, bf16[1024,128]{1,0:T(8,128)(2,1)}, u32[]{:S(2)}) copy-start(bf16[1024,128]{1,0:T(8,128)(2,1)} %v_ref.1) | copy-start | bytes 786436
  0.7 88.9 %copy-start.3 = (bf16[1024,128]{1,0:T(8,128)(2,1)S(1)}, bf16[1024,128]{1,0:T(8,128)(2,1)}, u32[]{:S(2)}) copy-start(bf16[1024,128]{1,0:T(8,128)(2,1)} %g_ref.1) | copy-start | bytes 786436
  0.7 88.9 %copy-start.6 = (s32[1,1024]{1,0:T(1,128)S(1)}, s32[1,1024]{1,0:T(1,128)}, u32[]{:S(2)}) copy-start(s32[1,1024]{1,0:T(1,128)} %owner_ref.1) | copy-start | bytes 12292
  88.9 0.7 copy-start.4
  88.9 0.6 copy-start.7
  88.9 0.7 copy-start.5

commit v6 on v5

--- a/solution.py
+++ b/solution.py
@@ -19,6 +19,7 @@
 CHUNK = PLANE * ROOM
 BLOCKS = TOK // 128
 ORDER = (4, 3, 5, 2, 6, 1, 7, 0)
+LATE = (4, 3, 5, 0, 2, 6, 1, 7)
 SEATS = 24
 EXTRA = 8
 PARTS = 4
@@ -387,6 +388,7 @@
     def signal(sem, k, j):
         pl.semaphore_signal(sem, inc=1, device_id={"seq": peer_at(k, j)}, device_id_type=MESH)
 
+    rmeta[...] = jnp.zeros_like(rmeta)
     loads = [
         pltpu.make_async_copy(ref, rows_in.at[:, pl.ds(HD * f, HD)], load_sem.at[f])
         for f, ref in enumerate((q_ref, k_ref, v_ref, g_ref))
@@ -415,10 +417,14 @@
         index, src, dst, sem, low, count = kinds[kind]
         some = pl.ds(low, count)
 
+        half = pl.ds(pl.multiple_of(my_place // 4 * 128, 128), 128)
+
         def body(j, carry):
             peer = peer_at(k, j)
+            key = kind == "meta"
             pltpu.make_async_remote_copy(
-                src_ref=src.at[peer, some], dst_ref=dst.at[me, some],
+                src_ref=src.at[peer, some, half] if key else src.at[peer, some],
+                dst_ref=dst.at[me, some, half] if key else dst.at[me, some],
                 send_sem=send_sem.at[index], recv_sem=sem.at[my_plane],
                 device_id={"seq": peer}, device_id_type=MESH,
             ).start()
@@ -433,12 +439,16 @@
         _, _, dst, sem, low, count = kinds[kind]
         p = lax.rem(my_plane + k, PLANES)
         some = dst.at[pl.ds(p * PLANE, PLANE - 1 if k == 0 else PLANE), pl.ds(low, count)]
+        if kind == "meta":
+            some = some.at[:, :, pl.ds(0, 128)]
         pltpu.make_async_copy(some, some, sem.at[p]).wait()
         return p
 
     def sent(kind):
         index, src, _, _, low, count = kinds[kind]
         some = src.at[pl.ds(0, DEVS - 1), pl.ds(low, count)]
+        if kind == "meta":
+            some = some.at[:, :, pl.ds(0, 128)]
         pltpu.make_async_copy(some, some, send_sem.at[index]).wait()
 
     ones = {
@@ -530,9 +540,10 @@
         key = label * UNIT + 32.0 * found[n : 2 * n] + found[2 * n :]
         return key + jnp.where(label > 0.0, here, 0.0)
 
-    lane = jnp.where(direct, rank + (my_place * SEATS).astype(F32), -1.0)
+    tile = my_place // 4 * 128
+    lane = jnp.where(direct, rank + (tile + lax.rem(my_place, 4) * SEATS).astype(F32), -1.0)
     key = keys_of(iota((DEVS, TOK), 0) == target, local + 1.0, iota((256, TOK), 0) == lane)
-    key = jnp.where(iota((DEVS, 256), 1) == 255.0, lost, key)
+    key = jnp.where(iota((DEVS, 256), 1) == (tile + 127).astype(F32), lost, key)
     smeta[...] = key.reshape(DEVS, 1, 256)
     first_lane = my_plane * EXTRA + lax.rem(my_place, 2) * 64
     lane = jnp.where(fits, extra + first_lane.astype(F32), -1.0)
@@ -543,7 +554,7 @@
     column("mx")
     rmx[my_place, my_plane] = smx[my_plane]
     pl.semaphore_wait(column_sem, PLANE - 1)
-    for k in ORDER:
+    for k in LATE:
         start_plane("meta", k)
     for k in ORDER[:3]:
         start("qk", k, 1, PLANE)
@@ -556,7 +567,7 @@
         start("qk", k, 1, PLANE)
         across("fx", True, first, last)
     for kind in ("v", "g"):
-        for k in ORDER:
+        for k in LATE:
             start(kind, k, 1, PLANE)
 
     slot_cols = turned(jnp.concatenate([slot[:, 128 * b : 128 * (b + 1)] for b in range(8)], axis=0))
@@ -569,10 +580,10 @@
 
     lax.fori_loop(0, PLANES, build_final, 0)
 
-    for k in ORDER:
+    for k in LATE:
         arrived("meta", (PLANES - k) % PLANES)
     got = jnp.sum(rmeta[...].reshape(PLANES, PLANE, 256), axis=1)
-    lost_any = jnp.max(got[:, 255:256], axis=0, keepdims=True)
+    lost_any = jnp.max(got[:, 127:128] + got[:, 255:256], axis=0, keepdims=True)
     sflag[0] = jnp.broadcast_to(lost_any, (1, 128))
     for i in range(1, PARTS):
         pltpu.make_async_remote_copy(
@@ -588,8 +599,7 @@
     mine = (got_extra >= UNIT) & (got_extra < (1.0 + CL_DEV) * UNIT)
     got_extra = jnp.where(mine, got_extra, 0.0)
     got_extra = jnp.sum(got_extra.reshape(PLANE // 2, 2, 128), axis=1)
-    tail = jnp.where(iota((PLANES, 128), 1) < 64.0, got[:, 128:], 0.0)
-    keys_all = jnp.concatenate([got[:, :128], tail, got_extra], axis=0)
+    keys_all = jnp.concatenate([got[:, :128], got[:, 128:], got_extra], axis=0)
     keys_all = jnp.where(keys_all < UNIT, NONE, keys_all)
     key_cols = turned(keys_all)
     n_rows = 2 * PLANES + PLANE // 2
@@ -621,18 +631,15 @@
             jnp.sum(jnp.where(at == p + PLANES * h, place, 0.0), axis=0, keepdims=True)
             for h in range(2)
         )
-        gather[p] = onehot(
-            jnp.concatenate(
-                [iota((TOK, 128), 0) == first, iota((TOK, 128), 0) == second], axis=1
-            )
-        )
+        both = jnp.concatenate([first[:, :96], second[:, :96]], axis=1)
+        gather[p] = onehot(iota((TOK, PLANE * SEATS), 0) == both)
         at = lax.broadcasted_iota(jnp.int32, (128, 128), 1)
         first, second = (
             jnp.sum(jnp.where(at == p + PLANES * h, place_cols, 0.0), axis=1, keepdims=True)
             for h in range(2)
         )
-        ungather[p, 0:128] = onehot(iota((128, TOK), 1) == first)
-        ungather[p, 128:192] = onehot(iota((64, TOK), 1) == second[:64])
+        ungather[p, 0:96] = onehot(iota((96, TOK), 1) == first[:96])
+        ungather[p, 96:192] = onehot(iota((96, TOK), 1) == second[:96])
         return carry
 
     lax.fori_loop(0, PLANES, build, 0)
@@ -659,10 +666,10 @@
     def collect(kind, features, cut):
         width = HD * len(features)
         acc[:, :width] = dot(xgather[...], extras(rx, features))
-        for k in ORDER:
+        for k in LATE:
             p = arrived(kind, (PLANES - k) % PLANES)
-            part = dot(gather[p, :, : PLANE * SEATS], together(cut(pl.ds(p * PLANE, PLANE))))
-            if k == ORDER[-1]:
+            part = dot(gather[p], together(cut(pl.ds(p * PLANE, PLANE))))
+            if k == LATE[-1]:
                 return acc[:, :width] + part
             acc[:, :width] += part
 
@@ -711,7 +718,7 @@
     ]
     outs = jnp.concatenate(attn, axis=0)
     res[:, :HD] = outs
-    for k in ORDER:
+    for k in LATE:
         p = lax.rem(my_plane + k, PLANES)
         block = dot(ungather[p], outs).reshape(PLANE, SEATS, HD)
         sa[pl.ds(p * PLANE, PLANE)] = block[:, :16].astype(BF16)
@@ -727,7 +734,7 @@
         value_tail = dvals[128:]
     res[pl.ds(128 * (BLOCKS - 1), 128), 3 * HD :] = value_tail.astype(BF16)
 
-    for k in ORDER:
+    for k in LATE:
         p = lax.rem(my_plane + k, PLANES)
         parts = [
             dot(ungather[p], res[:, at]).reshape(PLANE, SEATS, HD)
@@ -757,7 +764,7 @@
     last = pl.ds(128 * (BLOCKS - 1), 128)
     res[last, 2 * HD : 3 * HD] = key_tail.astype(BF16)
 
-    for i, k in enumerate(ORDER):
+    for i, k in enumerate(LATE):
         if i == 2:
             back = dot(xungather[...], res[...])
             back = [
@@ -796,12 +803,12 @@
         return [outs, keys[:, :SEATS], keys[:, SEATS:], rest[:, SEATS - 16 :]]
 
     for kind in ("a", "c"):
-        for k in ORDER:
+        for k in LATE:
             arrived(kind, (PLANES - k) % PLANES)
-    for k in ORDER:
+    for k in LATE:
         p = arrived("d", (PLANES - k) % PLANES)
         part = dot(final[p, :, : PLANE * SEATS], together(cut_back(pl.ds(p * PLANE, PLANE))))
-        if k == ORDER[0]:
+        if k == LATE[0]:
             acc[...] = part
         else:
             acc[...] += part
@@ -899,7 +906,7 @@
             extra_rows, extra_rows,
             *pair(4 * EXTRA, HD, PLANES),
             *pair(1, 128, PARTS, F32),
-            pltpu.VMEM((PLANES, TOK, 256), BF16),
+            pltpu.VMEM((PLANES, TOK, PLANE * SEATS), BF16),
             pltpu.VMEM((PLANES, PLANE * SEATS, TOK), BF16),
             pltpu.VMEM((PLANES, TOK, 256), BF16),
             pltpu.VMEM((TOK, DEVS * EXTRA), BF16),

time: 91.2 us -> 90.8 us (level)
  no operation moved by 1% of the time
where the time goes in v6:
time: 90.8 us; the launch traced here: 90.6 us
  Pallas kernels  88.8 us (98%)
    pallas_call x1, Pallas kernels, shards(): pl.pallas_call(kernel_fast, out_shape=out_shape + (jax.ShapeDtypeStruct((...  87.8 us

profile of v6, /device:TPU:1, one launch (start us, length us, event | category | flops | bytes accessed | tf_op | source)
XLA Modules:
  0.0 90.6 jit_solution(15374550111792356355)
XLA Ops:
  0.6 0.0 copy-start
  0.6 0.0 copy-start.1
  0.7 0.0 copy-start.2
  0.7 0.0 copy-start.3
  0.7 0.0 copy-start.6
  0.7 87.8 %shard_map.110 = (bf16[1024,128]{1,0:T(8,128)(2,1)S(1)}, bf16[1024,128]{1,0:T(8,128)(2,1)S(1)}, bf16[1024,128]{1,0:T(8,128)(2,1)S(1)}, bf16[1024,128]{1,0:T(8,12...) custom-call(bf16[1024,128]{1,0:T(8,128)(2,1)} %q_ref.1, bf16[1024,128]{1,0:T(8,128)(2,1)} %k_ref.1, ...), custom_call_target="tpu_custom_call" | custom-call | tf_op jit(solution)/shard_map/pallas_call | solution.py:891
  88.5 0.0 copy-start.4
  88.5 0.0 copy-start.7
  88.5 0.0 copy-start.5
  88.5 0.6 copy-done.7
  89.1 0.0 copy-done
  89.2 0.0 copy-done.1
  89.2 0.0 copy-done.2
  89.2 0.0 copy-done.3
  89.2 0.0 copy-done.6
  89.2 0.0 copy-done.4
  89.2 0.0 copy-done.5
  89.2 0.3 conditional.1
  89.5 1.0 %shard_map.111 = (bf16[1024,128]{1,0:T(8,128)(2,1)}, bf16[1024,128]{1,0:T(8,128)(2,1)}, bf16[1024,128]{1,0:T(8,128)(2,1)}, bf16[1024,128]{1,0:T(8,128)(2,1)}, f32[16,128]{1,0:T(8,128)}) custom-call(bf16[1024,128]{1,0:T(8,128)(2,1)S(1)} %get-tuple-element.58.refs_0_, bf16[1024,128]{1,0:T(8,128)(2,1)S(1)} %get-tuple-element.59.refs_1_, ...), custom_call_target="tpu_custom_call" | custom-call | tf_op jit(solution)/shard_map/pallas_call | solution.py:928
Async XLA Ops:
  0.6 88.5 %copy-start = (bf16[1024,128]{1,0:T(8,128)(2,1)S(1)}, bf16[1024,128]{1,0:T(8,128)(2,1)}, u32[]{:S(2)}) copy-start(bf16[1024,128]{1,0:T(8,128)(2,1)} %q_ref.1) | copy-start | bytes 786436
  0.6 88.5 %copy-start.1 = (bf16[1024,128]{1,0:T(8,128)(2,1)S(1)}, bf16[1024,128]{1,0:T(8,128)(2,1)}, u32[]{:S(2)}) copy-start(bf16[1024,128]{1,0:T(8,128)(2,1)} %k_ref.1) | copy-start | bytes 786436
  0.7 88.5 %copy-start.2 = (bf16[1024,128]{1,0:T(8,128)(2,1)S(1)}, bf16[1024,128]{1,0:T(8,128)(2,1)}, u32[]{:S(2)}) copy-start(bf16[1024,128]{1,0:T(8,128)(2,1)} %v_ref.1) | copy-start | bytes 786436
  0.7 88.5 %copy-start.3 = (bf16[1024,128]{1,0:T(8,128)(2,1)S(1)}, bf16[1024,128]{1,0:T(8,128)(2,1)}, u32[]{:S(2)}) copy-start(bf16[1024,128]{1,0:T(8,128)(2,1)} %g_ref.1) | copy-start | bytes 786436
  0.7 88.5 %copy-start.6 = (s32[1,1024]{1,0:T(1,128)S(1)}, s32[1,1024]{1,0:T(1,128)}, u32[]{:S(2)}) copy-start(s32[1,1024]{1,0:T(1,128)} %owner_ref.1) | copy-start | bytes 12292
  88.5 0.7 copy-start.4
  88.5 0.6 copy-start.7
  88.5 0.7 copy-start.5
